TPU v7x, 32 devices: a whole 2x2x4 slice. The times are simulated.
32 devices in a mesh: ctx: 8 (over y, x, core), dp: 4 (over z).
Axes of the slice: x: 2, y: 2, z: 4, core: 2. Of those that a mesh axis runs over, the one named last changes fastest.
Arguments:
- query_in: bfloat16 [4096, 8192], P('ctx', 'dp'), may hold values from -6 to 6
- key_in: bfloat16 [4096, 8192], P('ctx', 'dp'), may hold values from -6 to 6
- value_in: bfloat16 [4096, 8192], P('ctx', 'dp'), may hold values from -280 to 280
- log_decay: float32 [64, 4096], P('dp', 'ctx'), may hold values from -0.8 to 0
- norm_gain: float32 [8192], P('dp'), may hold values from 0.25 to 1.75
- grad_out: bfloat16 [4096, 8192], P('ctx', 'dp'), may hold values from -6 to 6
Outputs:
- attended: bfloat16 [4096, 8192], P('ctx', 'dp')
- grad_query: bfloat16 [4096, 8192], P('ctx', 'dp')
- grad_key: bfloat16 [4096, 8192], P('ctx', 'dp')
- grad_value: bfloat16 [4096, 8192], P('ctx', 'dp')
- grad_gain: float32 [8192], P('dp')
All inputs are finite; a program needn't handle non-finite values.
Results may differ from a plain program's by a relative error of at most 0.011.
Values sent between devices are 32-bit elements; how exact they have to be, the bound alone decides.
No kernel may reach another device: no remote copies, remote signals or barrier semaphores. Data moves between devices by JAX's collectives and lax.ppermute only.
A program may use at most 128 MiB of HBM per device.

v0:
```python
import math

import jax
import jax.numpy as jnp
from jax import lax
from jax.sharding import PartitionSpec as P

BLOCK = 512


def entering(value, axis, join, neutral, backward):
    count, mine = (lax.axis_size(axis), lax.axis_index(axis))
    pieces = jax.tree.map(lambda part: lax.all_gather(part, axis), value)
    if backward:
        pieces = jax.tree.map(lambda part: part[::-1], pieces)
        mine = count - 1 - mine
    so_far = jax.tree.map(
        lambda part, zero: jnp.full_like(part, 0) + jnp.asarray(zero, part.dtype), value, neutral
    )

    def turn(position, so_far):
        longer = join(so_far, jax.tree.map(lambda part: part[position], pieces))
        return jax.tree.map(lambda new, old: jnp.where(position < mine, new, old), longer, so_far)

    return lax.fori_loop(0, count - 1, turn, so_far)


def chain_join(earlier, later):
    return (earlier[0] * later[0], later[0][:, None, None] * earlier[1] + later[1])


def split_product(form, left, state):
    high_part = state.astype(jnp.bfloat16)
    low_part = (state - high_part.astype(jnp.float32)).astype(jnp.bfloat16)
    first = jnp.einsum(form, left, high_part, preferred_element_type=jnp.float32)
    return first + jnp.einsum(form, left, low_part, preferred_element_type=jnp.float32)


def on_device(query_in, key_in, value_in, log_decay, norm_gain, grad_out):
    row_count = query_in.shape[0]
    head_count = log_decay.shape[0]
    head_width = query_in.shape[1] // head_count
    block_count = row_count // BLOCK
    shaped = (block_count, BLOCK, head_count, head_width)
    query_rows = query_in.reshape(shaped)
    key_rows = key_in.reshape(shaped)
    value_rows = value_in.reshape(shaped)
    within = jnp.transpose(
        jnp.cumsum(log_decay.reshape(head_count, block_count, BLOCK), axis=2), (1, 2, 0)
    )
    totals = within[:, -1, :]
    device_total = jnp.sum(totals, axis=0)
    decay_total = jnp.exp(device_total)
    within_heads = jnp.transpose(within, (0, 2, 1))
    causal_mask = jnp.arange(BLOCK)[:, None] >= jnp.arange(BLOCK)[None, :]
    decay_gap = within_heads[:, :, :, None] - within_heads[:, :, None, :]
    decay_weights = jnp.where(causal_mask, jnp.exp(jnp.where(causal_mask, decay_gap, 0.0)), 0.0)
    scores = jnp.einsum("nthd,nshd->nhts", query_rows, key_rows, preferred_element_type=jnp.float32)
    weighted = (scores * decay_weights).astype(jnp.bfloat16)
    local_mix = jnp.einsum(
        "nhts,nshj->nthj", weighted, value_rows, preferred_element_type=jnp.float32
    )
    tail_decay = jnp.exp(totals[:, None, :] - within)
    key_weighted = (key_rows.astype(jnp.float32) * tail_decay[..., None]).astype(jnp.bfloat16)
    block_states = jnp.einsum(
        "nshi,nshj->nhij", key_weighted, value_rows, preferred_element_type=jnp.float32
    )
    running = jnp.zeros_like(block_states[0])
    before = jnp.zeros_like(device_total)
    block_index = 0
    starts = running
    running = jnp.exp(totals[block_index])[:, None, None] * running + block_states[block_index]
    local_state = running
    incoming = entering(
        (decay_total, local_state),
        "ctx",
        chain_join,
        (jnp.ones_like(decay_total), jnp.zeros_like(local_state)),
        False,
    )[1]
    start_states = jnp.stack([starts + jnp.exp(before)[:, None, None] * incoming])
    within_exp = jnp.exp(within)[..., None]
    query_scaled = query_rows.astype(jnp.float32) * within_exp
    carried = within_exp * split_product("nthi,nhij->nthj", query_rows, start_states)
    raw_out = (carried + local_mix).reshape(row_count, -1)
    feature_total = head_count * head_width * lax.axis_size("dp")
    grad_float = grad_out.astype(jnp.float32)
    scaled_grad = grad_float * norm_gain
    square_sum, cross_sum = lax.psum(
        (jnp.sum(raw_out * raw_out, axis=1), jnp.sum(scaled_grad * raw_out, axis=1)), "dp"
    )
    inv_rms = lax.rsqrt(square_sum / feature_total + 1e-06)
    normed = raw_out * inv_rms[:, None]
    attended = (normed * norm_gain).astype(jnp.bfloat16)
    cubed = inv_rms * inv_rms * inv_rms
    grad_raw = (
        inv_rms[:, None] * scaled_grad
        - raw_out * cubed[:, None] * cross_sum[:, None] / feature_total
    ).astype(jnp.bfloat16)
    gain_part = jnp.sum(grad_float * normed, axis=0) / math.sqrt(row_count * lax.axis_size("ctx"))
    grad_rows = grad_raw.reshape(shaped)
    grad_scores = jnp.einsum(
        "nthj,nshj->nhts", grad_rows, value_rows, preferred_element_type=jnp.float32
    )
    grad_weighted = (grad_scores * decay_weights).astype(jnp.bfloat16)
    local_query = jnp.einsum(
        "nhts,nshi->nthi", grad_weighted, key_rows, preferred_element_type=jnp.float32
    )
    local_key = jnp.einsum(
        "nhts,nthi->nshi", grad_weighted, query_rows, preferred_element_type=jnp.float32
    )
    local_value = jnp.einsum(
        "nhts,nthj->nshj", weighted, grad_rows, preferred_element_type=jnp.float32
    )
    query_weighted = query_scaled.astype(jnp.bfloat16)
    back_blocks = jnp.einsum(
        "nuhi,nuhj->nhij", query_weighted, grad_rows, preferred_element_type=jnp.float32
    )
    afters = [None] * block_count
    after_sums = [None] * block_count
    running = jnp.zeros_like(back_blocks[0])
    behind = jnp.zeros_like(device_total)
    for block_index in reversed(range(block_count)):
        afters[block_index] = running
        after_sums[block_index] = behind
        running = jnp.exp(totals[block_index])[:, None, None] * running + back_blocks[block_index]
        behind = totals[block_index]
    back_in = entering(
        (decay_total, running),
        "ctx",
        chain_join,
        (jnp.ones_like(decay_total), jnp.zeros_like(running)),
        True,
    )[1]
    grad_gain = lax.psum(gain_part, "ctx")
    end_states = jnp.stack([afters[0] + jnp.exp(after_sums[0])[:, None, None] * back_in])
    query_carried = within_exp * split_product("nthj,nhij->nthi", grad_rows, start_states)
    key_carried = tail_decay[..., None] * split_product("nshj,nhij->nshi", value_rows, end_states)
    value_carried = tail_decay[..., None] * split_product("nshi,nhij->nshj", key_rows, end_states)
    grad_query = (query_carried + local_query).astype(jnp.bfloat16).reshape(row_count, -1)
    grad_key = (key_carried + local_key).astype(jnp.bfloat16).reshape(row_count, -1)
    grad_value = (value_carried + local_value).astype(jnp.bfloat16).reshape(row_count, -1)
    return (attended, grad_query, grad_key, grad_value, grad_gain)


def solution(mesh):
    in_specs = (
        P("ctx", "dp"),
        P("ctx", "dp"),
        P("ctx", "dp"),
        P("dp", "ctx"),
        P("dp"),
        P("ctx", "dp"),
    )
    out_specs = (P("ctx", "dp"), P("ctx", "dp"), P("ctx", "dp"), P("ctx", "dp"), P("dp"))
    return jax.shard_map(
        on_device, mesh=mesh, in_specs=in_specs, out_specs=out_specs, check_vma=False
    )
```

profile of v0, /device:TPU:0, one launch (start us, length us, event | category | flops | bytes accessed | tf_op | source)
XLA Modules:
  0.0 258.3 jit_solution(8996425418606870430)
XLA Ops:
  7.2 0.0 copy-start
  7.2 0.0 all-gather.6.cloned.1.call-start
  7.2 0.9 reshape.249
  8.2 1.2 reduce-window.6
  9.3 0.2 slice_reduce_fusion
  9.5 0.1 copy.154
  9.8 0.8 exponential_bitcast_fusion.1
  10.5 0.1 copy.157
  10.6 3.6 %copy.200 = bf16[64,8,16,128]{3,2,1,0:T(8,128)(2,1)} copy(bf16[64,8,16,128]{3,1,2,0:T(8,128)(2,1)} %bitcast.191) | data formatting | bytes 4194304
  14.2 4.3 %copy.156 = bf16[512,16,128]{0,2,1:T(8,128)(2,1)} copy(bf16[512,16,128]{2,1,0:T(8,128)(2,1)} %bitcast.197) | data formatting | bytes 4194304 | tf_op jit(solution)/shard_map/reshape | solution.py:46
  18.5 3.4 %fusion.31 = f32[16,128,128]{2,1,0:T(8,128)} fusion(bf16[512,16,128]{0,2,1:T(8,128)(2,1)} %copy.156, f32[512,16]{0,1:T(8,128)S(1)} %copy.157, f32[16]{0:T(128)S(1)} %exponential_multiply_fusion, bf16[512,2048]{1,0:T(8,128)(2,1)S(1)} %copy-done), kind=kOutput, calls=%fused_computation.52 | convolution fusion | flops 271843328 | bytes 5275712 | tf_op jit(solution)/shard_map/nshi,nshj->nhij/dot_general | solution.py:65
  21.9 0.0 all-gather.6.cloned.1.call-update
  21.9 0.0 all-gather.8.cloned.1.call-start
  22.0 3.9 %copy.196 = bf16[512,2048]{0,1:T(8,128)(2,1)} copy(bf16[512,2048]{1,0:T(8,128)(2,1)} %param.10) | data formatting | bytes 4194304 | tf_op jit(solution)/shard_map/reshape.28
  25.9 1.0 copy.155
  26.9 0.1 copy.195
  27.1 10.2 %all-gather = f32[8,1,16]{2,1,0:T(1,128)S(1)} all-gather(f32[1,1,16]{2,1,0:T(1,128)S(1)} %get-tuple-element.283), channel_id=2, replica_groups=mesh['ctx'=8,'dp'=4] {'ctx'}, dimensions={0}, use_global_device_ids=true | all-gather | bytes 576 | tf_op jit(solution)/shard_map/all_gather | solution.py:13
  37.2 0.1 iota_compare_fusion
  37.4 0.6 copy-done.8
  38.0 9.6 %multiply_convert_fusion.1 = bf16[16,512,512]{2,1,0:T(8,128)(2,1)} fusion(bf16[512,16,128]{0,2,1:T(8,128)(2,1)} %bitcast.179, f32[16,512]{1,0:T(8,128)S(1)} %bitcast_add_fusion.7, pred[512,512]{1,0:T(8,128)(4,1)S(1)} %iota_compare_fusion, bf16[512,2048]{1,0:T(8,128)(2,1)} %param.11), kind=kOutput, calls=%fused_computation.7 | convolution fusion | flops 1094713344 | bytes 12877824 | tf_op jit(solution)/shard_map/nthd,nshd->nhts/dot_general | solution.py:58
  47.5 31.6 %all-gather.6.cloned.1.call-done = f32[128,128,128]{2,1,0:T(8,128)} async-done(((f32[16,128,128]{2,1,0:T(8,128)}), f32[128,128,128]{2,1,0:T(8,128)}) %all-gather.6.cloned.1.call-update) | async-done | bytes 8388624 | tf_op jit(solution)/shard_map/all_gather | solution.py:13
  79.1 10.4 %while.28 = (s32[]{:T(128)}, f32[16,128,128]{2,1,0:T(8,128)S(1)}, s32[]{:T(128)}, f32[8,16]{1,0:T(8,128)S(1)}, f32[8,16,128,128]{3,2,1,0:T(8,128)}, /*index=5*/s32[]{:T(128)}, s32[]{:T(128)}) while((s32[]{:T(128)}, f32[16,128,128]{2,1,0:T(8,128)S(1)}, s32[]{:T(128)}, f32[8,16]{1,0:T(8,128)S(1)}, f32[8,16,128,128]{3,2,1,0:T(8,128)}, ...), condition=%wide.region_3.4_spmd.clone, body=%wide.region_2.3_spmd.clone.sunk | while | flops 1048580 | bytes 3146025 | solution.py:25
  79.1 1.5 fusion.72
  80.6 1.5 fusion.72
  82.1 1.5 fusion.72
  83.6 1.5 fusion.72
  85.1 1.5 fusion.72
  86.6 1.5 fusion.72
  88.1 1.5 fusion.72
  89.6 4.6 %fusion.44 = f32[16,128,512]{2,1,0:T(8,128)} fusion(bf16[512,16,128]{0,2,1:T(8,128)(2,1)} %bitcast.180, f32[16,128,128]{2,1,0:T(8,128)S(1)} %get-tuple-element.193), kind=kOutput, calls=%fused_computation.78 | convolution fusion | flops 268697600 | bytes 7340032 | tf_op jit(solution)/shard_map/nthi,nhij->nthj/dot_general | solution.py:35
  94.2 2.7 %fusion.47 = f32[16,128,512]{2,1,0:T(8,128)} fusion(bf16[512,16,128]{0,2,1:T(8,128)(2,1)S(1)} %bitcast.183, f32[16,128,128]{2,1,0:T(8,128)S(1)} %get-tuple-element.193), kind=kOutput, calls=%fused_computation.81 | convolution fusion | flops 269484032 | bytes 7340032 | tf_op jit(solution)/shard_map/nthi,nhij->nthj/dot_general | solution.py:36
  96.9 10.8 %multiply_reduce_fusion = (f32[512]{0:T(512)S(1)}, f32[1,512,16,128]{1,3,2,0:T(8,128)}) fusion(bf16[16,512,512]{2,1,0:T(8,128)(2,1)} %multiply_convert_fusion.1, f32[16,128,512]{2,1,0:T(8,128)} %fusion.44, f32[16,128,512]{2,1,0:T(8,128)} %fusion.47, f32[512,16]{0,1:T(8,128)S(1)} %copy.155, bf16[512,2048]{1,0:T(8,128)(2,1)S(1)} %copy-done), kind=kOutput, calls=%fused_computation.30 | convolution fusion | flops 1078984192 | bytes 23103488 | tf_op jit(solution)/shard_map/nhts,nshj->nthj/dot_general | solution.py:60
  107.7 5.4 %copy.168 = f32[512,2048]{1,0:T(8,128)} copy(f32[512,2048]{0,1:T(8,128)} %bitcast.192) | data formatting | bytes 8388608 | tf_op jit(solution)/shard_map/reshape | solution.py:85
  113.1 11.7 %psum.21 = f32[512]{0:T(512)S(1)} all-reduce(f32[512]{0:T(512)S(1)} %get-tuple-element.286), channel_id=1, replica_groups=mesh['ctx'=8,'dp'=4] {'dp'}, use_global_device_ids=true, to_apply=%region_5.6 | all-reduce | flops 512 | bytes 4096 | tf_op jit(solution)/shard_map/psum | solution.py:89
  124.7 4.1 %fusion.7 = (f32[2048]{0:T(1024)S(1)}, f32[512]{0:T(512)S(1)}) fusion(bf16[512,2048]{1,0:T(8,128)(2,1)} %param.15, f32[512,2048]{1,0:T(8,128)} %copy.168, f32[512]{0:T(512)S(1)} %get-tuple-element.285, f32[2048]{0:T(1024)S(1)} %copy-done.7), kind=kLoop, calls=%fused_computation.16 | loop fusion | flops 7337472 | bytes 6311936 | tf_op jit(solution)/shard_map/reduce_sum | solution.py:100
  128.9 8.6 %psum.22 = f32[512]{0:T(512)S(1)} all-reduce(f32[512]{0:T(512)S(1)} %get-tuple-element.257), channel_id=1, replica_groups=mesh['ctx'=8,'dp'=4] {'dp'}, use_global_device_ids=true, to_apply=%region_7.8 | all-reduce | flops 512 | bytes 4096 | tf_op jit(solution)/shard_map/psum | solution.py:89
  137.5 5.5 %fusion.5 = (bf16[512,2048]{1,0:T(8,128)(2,1)}, bf16[512,2048]{1,0:T(8,128)(2,1)}) fusion(bf16[512,2048]{1,0:T(8,128)(2,1)} %param.15, f32[512,2048]{1,0:T(8,128)} %copy.168, f32[512]{0:T(512)S(1)} %psum.22, f32[512]{0:T(512)S(1)} %get-tuple-element.284, f32[2048]{0:T(1024)S(1)} %copy-done.7, f32[512]{0:T(512)S(1)} %get-tuple-element.285), kind=kLoop, calls=%fused_computation.14 | loop fusion | flops 11534336 | bytes 10500096 | tf_op jit(solution)/shard_map/convert_element_type | solution.py:99
  143.0 3.9 %copy.197 = bf16[512,2048]{0,1:T(8,128)(2,1)} copy(bf16[512,2048]{1,0:T(8,128)(2,1)} %get-tuple-element.278) | data formatting | bytes 4194304 | tf_op jit(solution)/shard_map/reshape.45
  146.9 3.9 %fusion.30 = f32[16,128,128]{2,1,0:T(8,128)} fusion(bf16[512,16,128]{0,2,1:T(8,128)(2,1)} %bitcast.184, bf16[512,16,128]{0,2,1:T(8,128)(2,1)} %bitcast.181, f32[512,16]{0,1:T(8,128)S(1)} %copy.155, f32[16]{0:T(128)S(1)} %exponential_multiply_fusion), kind=kOutput, calls=%fused_computation.51 | convolution fusion | flops 271843328 | bytes 5275712 | tf_op jit(solution)/shard_map/nuhi,nuhj->nhij/dot_general | solution.py:116
  150.8 0.0 all-gather.8.cloned.1.call-update
  150.8 4.5 %fusion.46 = f32[16,128,512]{2,1,0:T(8,128)} fusion(bf16[512,16,128]{0,2,1:T(8,128)(2,1)} %bitcast.185, f32[16,128,128]{2,1,0:T(8,128)S(1)} %get-tuple-element.193), kind=kOutput, calls=%fused_computation.80 | convolution fusion | flops 269484032 | bytes 7340032 | tf_op jit(solution)/shard_map/nthj,nhij->nthi/dot_general | solution.py:36
  155.3 2.6 %fusion.42 = f32[16,128,512]{2,1,0:T(8,128)} fusion(bf16[512,16,128]{0,2,1:T(8,128)(2,1)S(1)} %bitcast.186, f32[16,128,128]{2,1,0:T(8,128)S(1)} %get-tuple-element.193), kind=kOutput, calls=%fused_computation.76 | convolution fusion | flops 268697600 | bytes 7340032 | tf_op jit(solution)/shard_map/nthj,nhij->nthi/dot_general | solution.py:35
  158.0 7.5 %multiply_convert_fusion = bf16[16,512,512]{2,1,0:T(8,128)(2,1)} fusion(bf16[512,16,128]{0,2,1:T(8,128)(2,1)S(1)} %bitcast.187, f32[16,512]{1,0:T(8,128)S(1)} %copy-done.9, pred[512,512]{1,0:T(8,128)(4,1)S(1)} %iota_compare_fusion, bf16[512,2048]{1,0:T(8,128)(2,1)S(1)} %copy-done), kind=kOutput, calls=%fused_computation.6 | convolution fusion | flops 1094713344 | bytes 12877824 | tf_op jit(solution)/shard_map/nthj,nshj->nhts/dot_general | solution.py:102
  165.5 10.0 %fusion.10 = bf16[1,512,16,128]{1,3,2,0:T(8,128)(2,1)} fusion(f32[16,128,512]{2,1,0:T(8,128)} %fusion.42, f32[16,128,512]{2,1,0:T(8,128)} %fusion.46, bf16[16,512,512]{2,1,0:T(8,128)(2,1)} %multiply_convert_fusion, bf16[512,16,128]{0,2,1:T(8,128)(2,1)S(1)} %copy-done.6, f32[512,16]{0,1:T(8,128)S(1)} %copy.155), kind=kOutput, calls=%fused_computation.24 | convolution fusion | flops 1077936128 | bytes 21004288 | tf_op jit(solution)/shard_map/nhts,nshi->nthi/dot_general | solution.py:106
  175.5 4.0 %copy.188 = bf16[512,2048]{1,0:T(8,128)(2,1)} copy(bf16[512,2048]{0,1:T(8,128)(2,1)} %bitcast.194) | data formatting | bytes 4194304
  179.5 13.5 %psum.23 = f32[2048]{0:T(1024)} all-reduce(f32[2048]{0:T(1024)S(1)} %broadcast_multiply_fusion), channel_id=1, replica_groups=mesh['ctx'=8,'dp'=4] {'ctx'}, use_global_device_ids=true, to_apply=%region_11.12 | all-reduce | flops 2048 | bytes 16384 | tf_op jit(solution)/shard_map/psum | solution.py:135
  193.0 11.3 %all-gather.8.cloned.1.call-done = f32[128,128,128]{2,1,0:T(8,128)} async-done(((f32[16,128,128]{2,1,0:T(8,128)}), f32[128,128,128]{2,1,0:T(8,128)}) %all-gather.8.cloned.1.call-update) | async-done | bytes 8388624 | tf_op jit(solution)/shard_map/all_gather | solution.py:13
  204.4 7.9 %rev.7 = f32[8,16,128,128]{3,2,1,0:T(8,128)} reverse(f32[8,16,128,128]{3,2,1,0:T(8,128)} %bitcast.196), dimensions={0} | reverse | bytes 16777216 | tf_op jit(solution)/shard_map/rev | solution.py:15
  212.2 10.5 %while.29 = (s32[]{:T(128)}, f32[16,128,128]{2,1,0:T(8,128)S(1)}, s32[]{:T(128)}, f32[8,16]{1,0:T(8,128)S(1)}, f32[8,16,128,128]{3,2,1,0:T(8,128)}, /*index=5*/s32[]{:T(128)}, s32[]{:T(128)}) while((s32[]{:T(128)}, f32[16,128,128]{2,1,0:T(8,128)S(1)}, s32[]{:T(128)}, f32[8,16]{1,0:T(8,128)S(1)}, f32[8,16,128,128]{3,2,1,0:T(8,128)}, ...), condition=%wide.region_9.10_spmd.clone, body=%wide.region_8.9_spmd.clone.sunk | while | flops 1048580 | bytes 3146025 | solution.py:25
  212.2 1.5 fusion.73
  213.7 1.5 fusion.73
  215.2 1.5 fusion.73
  216.7 1.5 fusion.73
  218.2 1.5 fusion.73
  219.7 1.5 fusion.73
  221.2 1.5 fusion.73
  222.7 2.5 fusion.13
  225.2 0.8 fusion.15
  226.0 2.9 %fusion.19 = f32[16,128,512]{2,1,0:T(8,128)} fusion(f32[16,128,128]{2,1,0:T(8,128)S(1)} %get-tuple-element.194, bf16[512,2048]{1,0:T(8,128)(2,1)S(1)} %copy-done), kind=kOutput, calls=%fused_computation.40 | convolution fusion | flops 269484032 | bytes 7340032 | tf_op jit(solution)/shard_map/nshj,nhij->nshi/dot_general | solution.py:36
  228.9 2.7 %fusion.21 = f32[16,128,512]{2,1,0:T(8,128)} fusion(f32[16,128,128]{2,1,0:T(8,128)S(1)} %get-tuple-element.194, bf16[512,2048]{1,0:T(8,128)(2,1)S(1)} %copy-done), kind=kOutput, calls=%fused_computation.42 | convolution fusion | flops 268697600 | bytes 7340032 | tf_op jit(solution)/shard_map/nshj,nhij->nshi/dot_general | solution.py:35
  231.7 2.7 %fusion.8 = bf16[1,512,16,128]{1,3,2,0:T(8,128)(2,1)} fusion(f32[16,128,512]{2,1,0:T(8,128)S(1)} %fusion.15, f32[16,128,512]{2,1,0:T(8,128)S(1)} %fusion.13, bf16[512,16,128]{0,2,1:T(8,128)(2,1)S(1)} %bitcast.188, bf16[16,512,512]{2,1,0:T(8,128)(2,1)S(1)} %bitcast.190, f32[512,16]{0,1:T(8,128)S(1)} %copy.157), kind=kOutput, calls=%fused_computation.18 | convolution fusion | flops 1077936128 | bytes 21004288 | tf_op jit(solution)/shard_map/nhts,nthj->nshj/dot_general | solution.py:112
  234.4 3.9 %copy.190 = bf16[512,2048]{1,0:T(8,128)(2,1)} copy(bf16[512,2048]{0,1:T(8,128)(2,1)} %bitcast.195) | data formatting | bytes 4194304
  238.3 9.2 %fusion.9 = bf16[1,512,16,128]{1,3,2,0:T(8,128)(2,1)} fusion(f32[16,128,512]{2,1,0:T(8,128)} %fusion.21, f32[16,128,512]{2,1,0:T(8,128)} %fusion.19, bf16[512,16,128]{0,2,1:T(8,128)(2,1)} %bitcast.182, bf16[16,512,512]{2,1,0:T(8,128)(2,1)} %multiply_convert_fusion, f32[512,16]{0,1:T(8,128)S(1)} %copy.157), kind=kOutput, calls=%fused_computation.21 | convolution fusion | flops 1077936128 | bytes 21004288 | tf_op jit(solution)/shard_map/nhts,nthi->nshi/dot_general | solution.py:109
  247.5 3.9 %copy.189 = bf16[512,2048]{1,0:T(8,128)(2,1)} copy(bf16[512,2048]{0,1:T(8,128)(2,1)} %bitcast.193) | data formatting | bytes 4194304
  (52 shorter events, 0.3 us)
Async XLA Ops:
  7.2 11.3 %copy-start = (bf16[512,2048]{1,0:T(8,128)(2,1)S(1)}, bf16[512,2048]{1,0:T(8,128)(2,1)}, u32[]{:S(2)}) copy-start(bf16[512,2048]{1,0:T(8,128)(2,1)} %param.12) | copy-start | bytes 6291460
  7.2 71.9 %all-gather.6.cloned.1.call-start = ((), (), s32[]{:S(2)}) async-start(), calls=%async_computation | async-start | bytes 9437184 | tf_op jit(solution)/shard_map/all_gather | solution.py:13
  21.9 182.5 %all-gather.8.cloned.1.call-start = ((), (), s32[]{:S(2)}) async-start(), calls=%async_computation.1 | async-start | bytes 9437184 | tf_op jit(solution)/shard_map/all_gather | solution.py:13
  37.3 0.6 copy-start.8
  89.6 4.6 %copy-start.2 = (bf16[512,2048]{0,1:T(8,128)(2,1)S(1)}, bf16[512,2048]{0,1:T(8,128)(2,1)}, u32[]{:S(2)}) copy-start(bf16[512,2048]{0,1:T(8,128)(2,1)} %copy.196) | copy-start | bytes 6291460
  107.7 17.0 %copy-start.7 = (f32[2048]{0:T(1024)S(1)}, f32[2048]{0:T(1024)}, u32[]{:S(2)}) copy-start(f32[2048]{0:T(1024)} %param.14) | copy-start | bytes 24580
  150.8 4.5 %copy-start.3 = (bf16[512,2048]{0,1:T(8,128)(2,1)S(1)}, bf16[512,2048]{0,1:T(8,128)(2,1)}, u32[]{:S(2)}) copy-start(bf16[512,2048]{0,1:T(8,128)(2,1)} %copy.197) | copy-start | bytes 6291460
  155.3 2.6 %copy-start.9 = (f32[16,512]{1,0:T(8,128)S(1)}, f32[16,512]{1,0:T(8,128)}, u32[]{:S(2)}) copy-start(f32[16,512]{1,0:T(8,128)} %copy-done.8) | copy-start | bytes 98308
  158.0 7.6 %copy-start.6 = (bf16[512,16,128]{0,2,1:T(8,128)(2,1)S(1)}, bf16[512,16,128]{0,2,1:T(8,128)(2,1)}, u32[]{:S(2)}) copy-start(bf16[512,16,128]{0,2,1:T(8,128)(2,1)} %copy.156) | copy-start | bytes 6291460
  204.4 7.9 %copy-start.1 = (f32[16,128,128]{2,1,0:T(8,128)S(1)}, f32[16,128,128]{2,1,0:T(8,128)}, u32[]{:S(2)}) copy-start(f32[16,128,128]{2,1,0:T(8,128)} %custom-call.1) | copy-start | bytes 3145732
  222.7 2.5 copy-start.5
  225.2 6.4 %slice-start = ((s8[8388608]{0:T(1024)(128)(4,1)}), s8[4194304]{0:T(1024)(128)(4,1)S(1)}, s32[]{:S(2)}) async-start(s8[8388608]{0:T(1024)(128)(4,1)} %bitcast.189), calls=%async_computation.2 | async-start | bytes 8388608
  226.0 5.6 %slice-start.1 = ((s8[8388608]{0:T(1024)(128)(4,1)}), s8[4194304]{0:T(1024)(128)(4,1)S(1)}, s32[]{:S(2)}) async-start(s8[8388608]{0:T(1024)(128)(4,1)} %bitcast.189), calls=%async_computation.3 | async-start | bytes 8388608
  228.9 2.8 %copy-start.4 = (bf16[512,2048]{0,1:T(8,128)(2,1)S(1)}, bf16[512,2048]{0,1:T(8,128)(2,1)}, u32[]{:S(2)}) copy-start(bf16[512,2048]{0,1:T(8,128)(2,1)} %copy.197) | copy-start | bytes 6291460
Sparse Core Ops, SparseCore 0:
  22.0 57.0 all-gather.5
  150.9 53.3 all-gather.7
where the time goes:
time: 260 us; the launch traced here: 258 us
  matrix products  80.5 us (31%)
  local copies, waits for them, and re-layouts  44 us (17%)
  blocking collectives  44 us (17%)
  waiting for transfers between devices  43 us (17%)
  other arithmetic  32.1 us (12%)
  between operations  14.3 us (6%)
    all_gather x2, waiting for transfers between devices, entering(): pieces = jax.tree.map(lambda part: lax.all_gather(part, axis), value)  42.9 us
    select_n x14, other arithmetic, turn(): jnp.where(position < mine, new, old)  20.4 us
    psum x2, blocking collectives, on_device(): lax.psum((jnp.sum(raw_out * raw_out, axis=1), jnp.sum(scaled_grad * raw_o...  20.3 us
    unnamed x28, local copies, waits for them, and re-layouts  16 us
    psum x1, blocking collectives, on_device(): grad_gain = lax.psum(gain_part, 'ctx')  13.5 us
    dot_general x4, matrix products, split_product(): jnp.einsum(form, left, low_part, preferred_element_type=jnp.float32)  12.6 us
    dot_general x1, matrix products, on_device(): jnp.einsum('nhts,nshj->nthj', weighted, value_rows, preferred_element_typ...  10.8 us
    dot_general x4, matrix products, split_product(): jnp.einsum(form, left, high_part, preferred_element_type=jnp.float32)  10.7 us
  transfers between devices with their start and end apart: 2, of which 2 were waited for; matrix products, arithmetic and copies ran while one was open for 17% of the time, Pallas kernels for 0%

commit v1 on v0

v1 whole, which is shorter than its diff:
```python
import functools
import math

import jax
import jax.numpy as jnp
from jax import lax
from jax.experimental import pallas as pl
from jax.experimental.pallas import tpu as pltpu
from jax.sharding import PartitionSpec as P

BLOCK = 512
MIDDLE = BLOCK // 2
WIDTH = 128
EXTRA = 8
F32 = jnp.float32
BF16 = jnp.bfloat16
VMEM_LIMIT = 14 * 1024 * 1024

NN = (((1,), (0,)), ((), ()))
NT = (((1,), (1,)), ((), ()))
TN = (((0,), (0,)), ((), ()))
EARLY = slice(0, MIDDLE)
LATE = slice(MIDDLE, BLOCK)


def mul(left, right, form):
    return lax.dot_general(left, right, form, preferred_element_type=F32)


def twin(left, right, first, second):
    none = jnp.zeros(first.shape, BF16)
    above = jnp.concatenate([first.astype(BF16), none], axis=1)
    below = jnp.concatenate([none, second.astype(BF16)], axis=1)
    return mul(jnp.concatenate([left, right], axis=1), jnp.concatenate([above, below], axis=0), NN)


def iota(shape, axis):
    return lax.broadcasted_iota(jnp.int32, shape, axis)


def rows_of(i):
    return slice(i * WIDTH, (i + 1) * WIDTH)


def states_in(ref):
    return ref.shape[0] // WIDTH


def lanes(i):
    return slice(i * WIDTH, (i + 1) * WIDTH)


def pieces(value):
    first = value.astype(BF16)
    value = value - first.astype(F32)
    second = value.astype(BF16)
    return first, second, (value - second.astype(F32)).astype(BF16)


def apart(body):
    pl.when(lax.axis_index("ctx") >= 0)(body)


def first_head(side, chunk, heads, chunk_heads):
    half = lax.rem(lax.axis_index("ctx"), 2)
    if side:
        half = 1 - half
    return half * (heads // 2) + chunk * chunk_heads


def wide(head, i, count=1):
    return pl.ds(pl.multiple_of((head + i) * WIDTH, WIDTH), count * WIDTH)


def turned_to(column_ref, head):
    return pltpu.roll(column_ref[...], lax.rem(WIDTH - head, WIDTH), 1)


def write_decays(decay, row_ref, column_ref, grown_ref, tail_ref, log_ref):
    heads = decay.shape[0]
    upto = jnp.where(iota((WIDTH, WIDTH), 0) <= iota((WIDTH, WIDTH), 1), 1.0, 0.0).astype(BF16)
    carry = jnp.zeros((heads, 1), F32)
    blocks = []
    for block in range(BLOCK // WIDTH):
        total = carry
        for piece in pieces(decay[:, lanes(block)]):
            total = total + mul(piece, upto, NN)
        carry = total[:, WIDTH - 1 :]
        row_ref[:, lanes(block)] = total
        padded = jnp.concatenate([total, jnp.zeros((WIDTH - heads, WIDTH), F32)], axis=0)
        blocks.append(jnp.transpose(padded))
    mine = iota((heads, WIDTH), 1) == lax.axis_index("ctx")
    log_ref[...] = jnp.where(mine, jnp.broadcast_to(carry, (heads, WIDTH)), 0.0)
    within = jnp.concatenate(blocks, axis=0)
    column_ref[...] = within
    grown_ref[...] = jnp.exp(within)
    tail_ref[...] = jnp.exp(within[BLOCK - 1 :] - within)


def write_states(head, chunk, tail_ref, key_ref, value_ref, state_ref):
    tail = turned_to(tail_ref, head)
    count = states_in(state_ref)
    for i in range(count):
        at = lanes(chunk * count + i)
        weighted = (key_ref[:, at].astype(F32) * tail[:, i : i + 1]).astype(BF16)
        state_ref[rows_of(i)] = mul(weighted, value_ref[:, at], TN)


PARTS = 2


def row_part(n):
    return pl.ds(n * (BLOCK // PARTS), BLOCK // PARTS)


def pulled(source, target, sems, heads, side):
    copies = []
    at = wide(first_head(side, 0, heads, 0), 0, heads // 2)
    for part in range(PARTS):
        rows = row_part(part)
        copy = pltpu.make_async_copy(source.at[rows, at], target.at[rows], sems.at[part])
        copy.start()
        copies.append(copy)
    return copies


def flushed(held_refs, out_refs, sems, heads, side, chunk):
    copies = []
    for n, (held, out) in enumerate(zip(held_refs, out_refs)):
        count = held.shape[1] // WIDTH
        at = wide(first_head(side, chunk, heads, count), 0, count)
        for part in range(PARTS):
            rows = row_part(part)
            copy = pltpu.make_async_copy(held.at[rows], out.at[rows, at], sems.at[n, part])
            copy.start()
            copies.append(copy)
    return copies


def half_of(rows, side):
    count = rows.shape[0] // 2
    half = lax.rem(lax.axis_index("ctx"), 2)
    in_first = (half if side else 1 - half).astype(F32)
    return in_first * rows[:count] + (1.0 - in_first) * rows[count:]


def first_kernel(
    decay_in, key_in, value_in, row_ref, column_ref, grown_ref, tail_ref, log_ref, key_ref, value_ref,
    own_key_ref, own_value_ref, state_ref, decay_ref, decay_sem, sems, *, heads
):
    chunk_heads = states_in(state_ref)
    decay_copy = pltpu.make_async_copy(decay_in, decay_ref, decay_sem.at[0])
    decay_copy.start()
    copies = []
    for side, targets in ((1, (key_ref, value_ref)), (0, (own_key_ref, own_value_ref))):
        for chunk in range(2 if side else 1):
            count = chunk_heads if side else heads // 2
            at = wide(first_head(side, chunk, heads, count), 0, count)
            here = slice(chunk * count * WIDTH, (chunk + 1) * count * WIDTH)
            for source, target in zip((key_in, value_in), targets):
                copy = pltpu.make_async_copy(source.at[:, at], target.at[:, here], sems.at[len(copies)])
                copy.start()
                copies.append(copy)
    decay_copy.wait()
    write_decays(decay_ref[...], row_ref, column_ref, grown_ref, tail_ref, log_ref)
    for copy in copies[:2]:
        copy.wait()
    write_states(first_head(1, 0, heads, 0), 0, tail_ref, key_ref, value_ref, state_ref)
    for copy in copies[2:]:
        copy.wait()


def state_kernel(tail_ref, key_ref, value_ref, *refs, heads, side, chunk, load_side):
    copies = []
    if load_side is None:
        state_ref = refs[-1]
    else:
        state_ref, target, sems = refs[-3:]
        copies = pulled(refs[0], target, sems, heads, load_side)
    head = first_head(side, chunk, heads, states_in(state_ref))

    @apart
    def _():
        write_states(head, chunk, tail_ref, key_ref, value_ref, state_ref)

    for copy in copies:
        copy.wait()


TURNED_STRIPS = ((slice(0, WIDTH), slice(0, MIDDLE)), (slice(WIDTH, MIDDLE), slice(WIDTH, MIDDLE)))


def shifted(part, block):
    return slice(part.start + block * MIDDLE, part.stop + block * MIDDLE)


def local_kernel(
    row_ref, column_ref, grown_ref, query_ref, key_ref, value_ref, *refs, heads, side, chunk, loading
):
    copies = []
    if loading:
        out_ref, query_out, turned_out, state_ref, weighted_ref, decay_ref, *targets, sems = refs[-9:]
        for n in range(2):
            copies += pulled(refs[0], targets[n], sems.at[n], heads, n)
    else:
        out_ref, query_out, turned_out, state_ref, weighted_ref, decay_ref = refs[-6:]
    chunk_heads = state_ref.shape[0]

    @apart
    def _():
        head = first_head(side, chunk, heads, chunk_heads)
        column = turned_to(column_ref, head)
        grown = turned_to(grown_ref, head)
        middle = column[MIDDLE - 1 : MIDDLE]
        upto = jnp.exp(jnp.minimum(middle - column[EARLY], 0.0))
        since = jnp.exp(jnp.minimum(column[LATE] - middle, 0.0))
        seen = (
            iota((WIDTH, MIDDLE), 1) >= iota((WIDTH, MIDDLE), 0),
            iota((WIDTH, WIDTH), 1) >= iota((WIDTH, WIDTH), 0),
        )

        def spread(i):
            at = lanes(chunk * chunk_heads + i)
            row = row_ref[pl.ds(head + i, 1), :]
            for block in range(2):
                for mask, (here, there) in zip(seen, TURNED_STRIPS):
                    rows, other = shifted(here, block), shifted(there, block)
                    gap = row[:, other] - column[rows, i : i + 1]
                    decay = jnp.where(mask, jnp.exp(jnp.minimum(gap, 0.0)), 0.0)
                    scores = mul(key_ref[rows, at], query_ref[other, at], NT)
                    weighted_ref[i, rows, there] = (scores * decay).astype(BF16)
                    decay_ref[i, rows, there] = decay.astype(BF16)

        def gather(i):
            at = lanes(chunk * chunk_heads + i)
            weighted_query = query_ref[:, at].astype(F32) * grown[:, i : i + 1]
            query_out[:, lanes(i)] = weighted_query.astype(BF16)
            turned_out[lanes(i), :] = jnp.transpose(weighted_query).astype(BF16)
            key = (key_ref[EARLY, at].astype(F32) * upto[:, i : i + 1]).astype(BF16)
            state = mul(key, value_ref[EARLY, at], TN).astype(BF16)
            state_ref[i] = state
            query = (query_ref[LATE, at].astype(F32) * since[:, i : i + 1]).astype(BF16)
            for block in range(2):
                first, second = (shifted(here, block) for here, _ in TURNED_STRIPS)
                both = slice(first.start, second.stop)
                terms = (
                    mul(weighted_ref[i, first, :WIDTH], value_ref[first, at], TN),
                    mul(weighted_ref[i, both, WIDTH:], value_ref[both, at], TN),
                )
                for rows, term in zip((first, second), terms):
                    if block:
                        term = term + mul(query[rows.start - MIDDLE : rows.stop - MIDDLE], state, NN)
                    out_ref[rows, lanes(i)] = term.astype(BF16)

        spread(0)
        for i in range(chunk_heads):
            if i + 1 < chunk_heads:
                spread(i + 1)
            gather(i)

    for copy in copies:
        copy.wait()


def raw_kernel(local_ref, query_ref, grad_ref, gain_ref, start_ref, *refs, heads, side, chunk, first, last):
    raw_ref, sums_ref = refs[-2:]
    count = states_in(start_ref)
    head = first_head(side, chunk, heads, count)
    squares = jnp.zeros((BLOCK, WIDTH), F32) if first else refs[0][0]
    crosses = jnp.zeros((BLOCK, WIDTH), F32) if first else refs[0][1]
    both = None
    for i in range(count):
        at = lanes(chunk * count + i)
        if i % 2:
            raw = both[:, WIDTH:]
        elif i + 1 < count:
            both = twin(
                query_ref[:, lanes(i)], query_ref[:, lanes(i + 1)], start_ref[rows_of(i)], start_ref[rows_of(i + 1)]
            )
            raw = both[:, :WIDTH]
        else:
            raw = mul(query_ref[:, lanes(i)], start_ref[rows_of(i)].astype(BF16), NN)
        raw = raw + local_ref[:, lanes(i)].astype(F32)
        raw_ref[:, lanes(i)] = raw.astype(BF16)
        squares = squares + raw * raw
        crosses = crosses + grad_ref[:, at].astype(F32) * gain_ref[0:1, wide(head, i)] * raw
    if last:
        sums_ref[0:1, :] = jnp.sum(jnp.transpose(squares), axis=0, keepdims=True)
        sums_ref[1:2, :] = jnp.sum(jnp.transpose(crosses), axis=0, keepdims=True)
    else:
        sums_ref[0] = squares
        sums_ref[1] = crosses


def back_kernel(turned_ref, raw_ref, grad_ref, gain_ref, sums_ref, *refs, heads, side, chunk, first, features):
    if first:
        out_ref, state_ref, norm_ref = refs[-3:]
        total = sums_ref[...] + refs[0][...]
        inverse = lax.rsqrt(total[0:1] / features + 1e-06)
        cross = inverse * inverse * inverse * total[1:2] / features
        norm_ref[0] = jnp.transpose(jnp.broadcast_to(inverse, (WIDTH, BLOCK)))
        norm_ref[1] = jnp.transpose(jnp.broadcast_to(cross, (WIDTH, BLOCK)))
    else:
        out_ref, state_ref = refs[-2:]
        norm_ref = sums_ref
    count = states_in(state_ref)
    head = first_head(side, chunk, heads, count)
    state_ref[count * WIDTH :] = jnp.zeros((EXTRA, WIDTH), F32)
    for i in range(count):
        raw = raw_ref[:, lanes(i)].astype(F32)
        cotangent = grad_ref[:, lanes(chunk * count + i)].astype(F32)
        grad = norm_ref[0] * (cotangent * gain_ref[0:1, wide(head, i)]) - raw * norm_ref[1]
        grad = grad.astype(BF16)
        out_ref[:, lanes(i)] = grad
        state_ref[rows_of(i)] = mul(turned_ref[lanes(i), :], grad, NN)
        terms = jnp.sum(cotangent * (raw * norm_ref[0]), axis=0, keepdims=True)
        state_ref[count * WIDTH + i : count * WIDTH + i + 1] = terms


def ready_kernel(column_ref, tail_ref, query_ref, key_ref, value_ref, *refs, heads, side, chunk):
    key_out, value_out, since_out = refs[-3:]
    chunk_heads = key_out.shape[1] // WIDTH
    head = first_head(side, chunk, heads, chunk_heads)
    column = turned_to(column_ref, head)
    tail = turned_to(tail_ref, head)
    since = jnp.exp(jnp.minimum(column[LATE] - column[MIDDLE - 1 : MIDDLE], 0.0))
    for i in range(chunk_heads):
        at = lanes(chunk * chunk_heads + i)
        query = query_ref[LATE, at].astype(F32) * since[:, i : i + 1]
        since_out[lanes(i), :] = jnp.transpose(query).astype(BF16)
        key_out[:, lanes(i)] = (key_ref[:, at].astype(F32) * tail[:, i : i + 1]).astype(BF16)
        value_out[:, lanes(i)] = (value_ref[:, at].astype(F32) * tail[:, i : i + 1]).astype(BF16)


def grad_kernel(
    column_ref, grown_ref, query_ref, key_ref, value_ref, grad_ref, raw_ref, gain_ref, norm_ref,
    start_ref, middle_ref, since_ref, weighted_ref, decay_ref, *refs, heads, side, chunk, done
):
    chunk_heads = weighted_ref.shape[0]
    head = first_head(side, chunk, heads, chunk_heads)
    if done is not None:
        query_all, attended_all, query_out, attended_out, key_out, value_out, spread_ref, sems = refs[-8:]
        copies = flushed(refs[:2], (query_all, attended_all), sems, heads, *done)
    else:
        query_out, attended_out, key_out, value_out, spread_ref = refs[-5:]
        copies = []
    @apart
    def _():
        column = turned_to(column_ref, head)
        grown = turned_to(grown_ref, head)
        middle = column[MIDDLE - 1 : MIDDLE]
        upto = jnp.exp(jnp.minimum(middle - column[EARLY], 0.0))
        since = jnp.exp(jnp.minimum(column[LATE] - middle, 0.0))

        def spread(i):
            at = lanes(chunk * chunk_heads + i)
            here = lanes(i)
            for block in range(2):
                for mine, others in TURNED_STRIPS:
                    rows, other = shifted(mine, block), shifted(others, block)
                    grad_scores = mul(value_ref[rows, at], grad_ref[other, here], NT)
                    grad_weighted = grad_scores * decay_ref[i, rows, others].astype(F32)
                    spread_ref[i % 2, rows, others] = grad_weighted.astype(BF16)

        def gather(i):
            at = lanes(chunk * chunk_heads + i)
            here = lanes(i)
            normed = raw_ref[:, here].astype(F32) * norm_ref[0]
            attended_out[:, here] = (normed * gain_ref[0:1, wide(head, i)]).astype(BF16)
            state = start_ref[rows_of(i)]
            half_state = grown[MIDDLE - 1 : MIDDLE, i : i + 1] * state + middle_ref[i].astype(F32)
            back = mul(since_ref[here, :], grad_ref[LATE, here], NN)
            ends = twin(value_ref[EARLY, at], key_ref[EARLY, at], jnp.transpose(back), back)
            carried = twin(
                grad_ref[EARLY, here], grad_ref[LATE, here], jnp.transpose(state), jnp.transpose(half_state)
            )
            for block in range(2):
                for mine, others in TURNED_STRIPS:
                    rows, other = shifted(mine, block), shifted(others, block)
                    grad_weighted = spread_ref[i % 2, rows, others]
                    grad_value = mul(weighted_ref[i, rows, others], grad_ref[other, here], NN)
                    grad_key = mul(grad_weighted, query_ref[other, at], NN)
                    if not block:
                        factor = upto[rows, i : i + 1]
                        grad_key = grad_key + factor * ends[rows, :WIDTH]
                        grad_value = grad_value + factor * ends[rows, WIDTH:]
                    key_out[rows, here] = grad_key.astype(BF16)
                    value_out[rows, here] = grad_value.astype(BF16)
                first, second = (shifted(mine, block) for mine, _ in TURNED_STRIPS)
                both = slice(first.start, second.stop)
                terms = (
                    mul(spread_ref[i % 2, first, :WIDTH], key_ref[first, at], TN),
                    mul(spread_ref[i % 2, both, WIDTH:], key_ref[both, at], TN),
                )
                for rows, term in zip((first, second), terms):
                    if block:
                        mine = slice(rows.start - MIDDLE, rows.stop - MIDDLE)
                        factor = since[mine, i : i + 1]
                    else:
                        mine = rows
                        factor = grown[rows, i : i + 1]
                    query_out[rows, here] = (term + factor * carried[mine, lanes(block)]).astype(BF16)

        spread(0)
        for i in range(chunk_heads):
            if i + 1 < chunk_heads:
                spread(i + 1)
            gather(i)

    for copy in copies:
        copy.wait()


def end_kernel(*refs, heads, spots, done, rest, scale):
    groups = [refs[5 * n : 5 * n + 5] for n in range(len(spots))]
    refs = refs[5 * len(spots) :]
    chunk_heads = states_in(groups[0][4])
    copies = []
    if done is not None:
        query_all, attended_all, key_all, value_all, key_out, value_out, sems, own_sems = refs[-8:]
        copies += flushed(refs[:2], (query_all, attended_all), sems, heads, *done)
    else:
        key_all, value_all, gain_out, key_out, value_out, own_sems = refs[-6:]
    size = chunk_heads
    for n, (key_ref, value_ref, key_part, value_part, end_ref) in enumerate(groups):
        head = first_head(*spots[n], heads, chunk_heads)
        for piece in range(chunk_heads // size):

            @apart
            def _():
                for i in range(piece * size, (piece + 1) * size):
                    here = lanes(i)
                    end = end_ref[rows_of(i)].astype(BF16)
                    key_term = mul(value_ref[:, here], end, NT)
                    key_out[n, :, here] = (key_term + key_part[:, here].astype(F32)).astype(BF16)
                    value_term = mul(key_ref[:, here], end, NN)
                    value_out[n, :, here] = (value_term + value_part[:, here].astype(F32)).astype(BF16)

            held = (key_out.at[n], value_out.at[n])
            copies += flushed(held, (key_all, value_all), own_sems.at[n], heads, *spots[n])
    if done is None:

        @apart
        def _():
            sources = [(spot, group[4]) for spot, group in zip(spots, groups)] + list(zip(rest, refs))
            for spot, source in sources:
                head = first_head(*spot, heads, chunk_heads)
                for i in range(chunk_heads):
                    at = chunk_heads * WIDTH + i
                    gain_out[pl.ds(head + i, 1), :] = source[at : at + 1] * scale

    for copy in copies:
        copy.wait()


def sum_kernel(left_ref, right_ref, *refs):
    refs[-1][...] = left_ref[...] + right_ref[...]


def pass_kernel(left_ref, right_ref, state_ref, *refs):
    refs[-2][...] = left_ref[...] + right_ref[...]
    refs[-1][...] = state_ref[...]


def blend_kernel(factor_ref, *refs, rows, first, inputs, outputs, plain):
    ins, outs = refs[:inputs], refs[len(refs) - outputs :]
    for which, out_ref in enumerate(outs):
        count = states_in(out_ref)
        for i in range(count):
            total = None
            for source, row in zip(ins, rows[which]):
                if row is None:
                    continue
                term = factor_ref[row, first + i : first + i + 1, :] * source[rows_of(i)]
                total = term if total is None else total + term
            out_ref[rows_of(i)] = total
        if out_ref.shape[0] > count * WIDTH:
            below = slice(count * WIDTH, None)
            out_ref[below] = ins[plain[0]][below] + ins[plain[1]][below]


def swap(value, axis, bit):
    return lax.ppermute(value, axis, [(i, i ^ bit) for i in range(lax.axis_size(axis))])


def butterfly(value, axis):
    bit = 1
    while bit < lax.axis_size(axis):
        value = value + swap(value, axis, bit)
        bit *= 2
    return value


def pair_bits(count):
    in_order = [2 << n for n in range((count // 2).bit_length() - 1)]
    return [(bit, other) for bit, other in zip(in_order, in_order[::-1] if count == 8 else in_order)]


def factor_kernel(*refs, parts, count, backward):
    out_ref = refs[-1]
    logs = refs[0][...]
    for ref in refs[1:parts]:
        logs = logs + ref[...]
    logs = half_of(logs, 0)
    device = lax.axis_index("ctx")
    half = lax.rem(device, 2)
    in_first = (1 - half).astype(F32)
    place = iota(logs.shape, 1)
    mine = device
    if backward:
        place = count - 1 - place
        mine = count - 1 - device
    late = lax.rem(mine, 2).astype(F32)
    pair = mine // 2
    one = jnp.ones_like(logs)

    def choose(condition, yes, no):
        chosen = condition.astype(F32) if condition.dtype == jnp.bool_ else condition
        return chosen * yes + (1.0 - chosen) * no

    def devices(low, high):
        inside = (place >= low) & (place < high)
        total = jnp.sum(jnp.where(inside, logs, 0.0), axis=1, keepdims=True)
        return jnp.exp(jnp.broadcast_to(total, logs.shape))

    def span(low, high):
        return devices(2 * low, 2 * high)

    early_decay = devices(2 * pair, 2 * pair + 1)
    late_decay = devices(2 * pair + 1, 2 * pair + 2)
    rows = [choose(late, one, late_decay), choose(late, late_decay, one)]
    sent = one
    stages = []
    for bit, _ in pair_bits(count):
        size = bit // 2
        low = pair // size * size
        odd = lax.rem(pair // size, 2)
        other = low + size - 2 * odd * size
        later = odd.astype(F32)
        stages.append((
            later * span(low, pair),
            choose(later, one, span(other, other + size)),
            choose(later, span(low, low + size), one),
        ))
    if count == 8:
        high, low = pair // 2, lax.rem(pair, 2)
        below = high.astype(F32)
        sent = in_first * one + (1.0 - in_first) * span(pair + 1, 2 * high + 2)
        across = [
            (below * span(2 * high, pair), (1.0 - low.astype(F32)) * one, below * span(pair, 2 * high + 1)),
            (one, 0.0 * one, 0.0 * one),
        ]
        stages = [
            tuple(in_first * x + (1.0 - in_first) * y for x, y in zip(plain, other))
            for plain, other in zip(stages, across)
        ]
    rows += [sent * rows[0], sent * rows[1]]
    for _, keep, add in stages:
        rows += [keep, add]
    own_factor = choose(late, early_decay, one)
    given_factor = choose(late, one, early_decay)
    rows += [own_factor * take for take, _, _ in stages] + [late * one]
    rows += [given_factor * take for take, _, _ in stages] + [(1.0 - late) * one]
    for n, row in enumerate(rows):
        out_ref[n] = row


def on_device(query_in, key_in, value_in, log_decay, norm_gain, grad_out):
    heads = log_decay.shape[0]
    half_heads = heads // 2
    chunks = 2
    chunk_heads = half_heads // chunks
    shards = lax.axis_size("dp")
    count = lax.axis_size("ctx")
    features = heads * WIDTH * shards
    positions = BLOCK * count
    gain = norm_gain.reshape(1, -1)
    bits = pair_bits(count)
    stages = len(bits)

    vmem_spec = pl.BlockSpec(memory_space=pltpu.VMEM)
    any_spec = pl.BlockSpec(memory_space=pl.ANY)

    def held(shape, dtype=BF16):
        return pltpu.VMEM(shape, dtype)

    part = (BLOCK, chunk_heads * WIDTH)
    half_shape = (BLOCK, half_heads * WIDTH)
    state_shape = (chunk_heads * WIDTH, WIDTH)
    long_shape = (chunk_heads * WIDTH + EXTRA, WIDTH)
    column_shape = (BLOCK, WIDTH)
    table_shape = (chunk_heads, BLOCK, MIDDLE)
    result = pltpu.HBM((BLOCK, heads * WIDTH), BF16)

    def call(body, name, ins, outs, far=(), scratch=(), after=(), into=()):
        near = [pltpu.with_memory_space_constraint(value, pltpu.VMEM) for value in ins]
        far = [pltpu.with_memory_space_constraint(value, pltpu.HBM) for value in list(far) + list(into)]
        aliases = {len(near) + len(far) - len(into) + n: n for n in range(len(into))}
        extra = far + list(after)
        return pl.pallas_call(
            body,
            name=name,
            in_specs=[vmem_spec] * len(near) + [any_spec] * len(extra),
            out_specs=[any_spec if out is result else vmem_spec for out in outs],
            out_shape=list(outs),
            scratch_shapes=list(scratch),
            input_output_aliases=aliases,
            compiler_params=pltpu.CompilerParams(vmem_limit_bytes=VMEM_LIMIT),
            cost_estimate=pl.CostEstimate(flops=10000, bytes_accessed=1024, transcendentals=0),
        )(*near, *extra)

    class Scan:
        def __init__(self, shape, opened):
            self.shape = held(shape, F32)
            self.opened = [held(shape, F32) for shape in opened]
            self.arrived = [[] for _ in range(chunks)]
            self.received, self.own, self.message = ({}, {}, {})

        def blend(self, chunk, factors, ins, rows, plain, after, shape=None):
            body = functools.partial(
                blend_kernel, rows=rows, first=chunk * chunk_heads, inputs=len(ins), outputs=len(rows),
                plain=plain,
            )
            return call(body, "blend", [factors, *ins], [shape or self.shape] * len(rows), after=after)

        def send(self, chunk, state):
            self.received[chunk] = swap(state, "ctx", 1)

        def forward(self, chunk, message, sent=None):
            plain, other = bits[len(self.arrived[chunk])]
            pairs = [(i, i ^ (other if i % 2 else plain)) for i in range(count)]
            self.message[chunk] = message
            self.arrived[chunk].append(lax.ppermute(message if sent is None else sent, "ctx", pairs))

        def open(self, chunk, factors, state, after=()):
            self.own[chunk] = state
            ins = [state, self.received[chunk]]
            message, sent = self.blend(chunk, factors, ins, [[0, 1], [2, 3]], (0, 1), after, self.opened[chunk])
            self.message[chunk] = message
            if stages:
                self.forward(chunk, message, sent)
            return message

        def step(self, chunk, factors, after=()):
            at = 2 + 2 * len(self.arrived[chunk])
            ins = [self.message[chunk], self.arrived[chunk][-1]]
            message = self.blend(chunk, factors, ins, [[at, at + 1]], (0, 1), after)[0]
            self.forward(chunk, message)
            return message

        def close(self, chunk, factors, after=()):
            at = 4 + 2 * stages
            ins = self.arrived[chunk] + [self.received[chunk], self.own[chunk], self.message[chunk]]
            own_rows = list(range(at, at + stages)) + [at + stages, None, None]
            at += stages + 1
            given_rows = list(range(at, at + stages)) + [None, at + stages, None]
            plain = (stages - 1, stages + 2) if stages else (0, 1)
            own, given = self.blend(chunk, factors, ins, [own_rows, given_rows], plain, after)
            return own, swap(given, "ctx", 1), given

    own, other = 0, 1
    order = [(side, chunk) for side in (own, other) for chunk in range(chunks)]
    spots = {(side, chunk): dict(heads=heads, side=side, chunk=chunk) for side, chunk in order}
    ahead = Scan(state_shape, [state_shape] * chunks)
    behind = Scan(long_shape, [long_shape] * chunks)
    factor_rows = 6 + 4 * stages

    def factors_of(logs, backward, after=()):
        body = functools.partial(factor_kernel, parts=len(logs), count=count, backward=backward)
        return call(body, "factors", logs, [held((factor_rows, half_heads, WIDTH), F32)], after=after)[0]

    def total(left, right, after):
        return call(sum_kernel, "sums", [left, right], [held(left.shape, F32)], after=after)[0]

    keys, values, queries, cotangents, states = ({}, {}, {}, {}, {})
    pull_sems = pltpu.SemaphoreType.DMA((2, PARTS))
    (row_values, column_values, grown, tails, placed, keys[other], values[other], keys[own], values[own],
     states[other, 0]) = call(
        functools.partial(first_kernel, heads=heads), "first_state", [],
        [held((heads, BLOCK), F32)] + [held(column_shape, F32)] * 3
        + [held((heads, WIDTH), F32)] + [held(half_shape)] * 4 + [held(state_shape, F32)],
        [log_decay, key_in, value_in],
        [pltpu.VMEM((heads, BLOCK), F32), pltpu.SemaphoreType.DMA((1,)), pltpu.SemaphoreType.DMA((6,))],
    )

    def state_call(side, chunk, load_side, after):
        loads = [] if load_side is None else [query_in]
        states[side, chunk], *loaded = call(
            functools.partial(state_kernel, load_side=load_side, **spots[side, chunk]),
            "local_state", [tails, keys[side], values[side]],
            [held(state_shape, F32)] + [held(half_shape) for _ in loads], loads,
            [pltpu.SemaphoreType.DMA((PARTS,)) for _ in loads], after,
        )
        for array in loaded:
            queries[load_side] = array
        return (states[side, chunk],)

    reach = [2] if count == 8 else [2 << n for n in range(stages)]
    logs = placed
    there = swap(logs, "ctx", reach[0]) if reach else None
    ahead.send(0, states[other, 0])
    last = state_call(other, 1, own, (states[other, 0],))
    last = state_call(own, 0, None, last)
    for bit in reach[1:]:
        logs = total(logs, there, last)
        there = swap(logs, "ctx", bit)
    sent = states[other, 1]
    if reach:
        logs, sent = call(
            pass_kernel, "logs", [logs, there, sent], [held(logs.shape, F32), held(state_shape, F32)], after=last
        )
        last = (logs,)
    ahead.send(1, sent)
    all_logs = [logs, swap(logs, "ctx", 1)]
    last = state_call(own, 1, other, last)
    factors = factors_of(all_logs, False, last)
    last = (ahead.open(0, factors, states[own, 0]),)
    last = (ahead.open(1, factors, states[own, 1], last),)

    locals_, ready = ({}, {})

    def local_call(side, chunk, after):
        loading = not cotangents
        outs = call(
            functools.partial(local_kernel, loading=loading, **spots[side, chunk]), "local_mix",
            [row_values, column_values, grown, queries[side], keys[side], values[side]],
            [held(part), held(part), held((chunk_heads * WIDTH, BLOCK)), held((chunk_heads, WIDTH, WIDTH)),
             held(table_shape), held(table_shape)] + [held(half_shape)] * (2 * loading),
            [grad_out] * loading, [pull_sems] * loading, after,
        )
        if loading:
            cotangents[own], cotangents[other] = outs[6:]
        locals_[side, chunk] = outs[:6]
        return (outs[0],)

    def ready_call(side, chunk, after):
        ready[side, chunk] = call(
            functools.partial(ready_kernel, **spots[side, chunk]), "weighted",
            [column_values, tails, queries[side], keys[side], values[side]],
            [held(part), held(part), held((chunk_heads * WIDTH, MIDDLE))], after=after,
        )
        return (ready[side, chunk][0],)

    to_mix, to_ready = list(order), list(order)
    last = local_call(*to_mix.pop(0), last)
    for stage in range(1, stages):
        for chunk in range(chunks):
            last = (ahead.step(chunk, factors, last),)
            if to_mix:
                last = local_call(*to_mix.pop(0), last)
    back_factors = factors_of(all_logs, True, last)
    last = (back_factors,)
    starts, raws = ({}, {})
    sums = []

    def raw_call(side, chunk, after):
        nonlocal sums
        final = (side, chunk) == order[-1]
        raws[side, chunk], sums_out = call(
            functools.partial(raw_kernel, first=not sums, last=final, **spots[side, chunk]), "raw_out",
            [*locals_[side, chunk][:2], cotangents[side], gain, starts[side, chunk]] + sums,
            [held(part), held((2, BLOCK) if final else (2, BLOCK, WIDTH), F32)], after=after,
        )
        sums = [sums_out]
        return (sums_out,)

    for chunk in range(chunks):
        starts[own, chunk], starts[other, chunk], given = ahead.close(chunk, factors, last)
        last = raw_call(own, chunk, (given,))
        while to_mix:
            last = local_call(*to_mix.pop(0), last)
    for chunk in range(chunks):
        last = raw_call(other, chunk, last)
    sums = sums[0]

    arrived = None
    bit = 1
    while bit < shards:
        if arrived is not None:
            sums = total(sums, arrived, last)
            last = (sums,)
        arrived = swap(sums, "dp", bit)
        for _ in range(2):
            if to_ready:
                last = ready_call(*to_ready.pop(0), last)
        bit *= 2
    if arrived is None:
        arrived = jnp.zeros_like(sums)

    grads = {}
    norms = None
    for side, chunk in [(other, chunk) for chunk in range(chunks)] + [(own, chunk) for chunk in range(chunks)]:
        first = norms is None
        grads[side, chunk], state, *more = call(
            functools.partial(back_kernel, features=features, first=first, **spots[side, chunk]), "grad_raw",
            [locals_[side, chunk][2], raws[side, chunk], cotangents[side], gain]
            + ([sums, arrived] if first else [norms]),
            [held(part), held(long_shape, F32)] + [held((2, BLOCK, WIDTH), F32)] * first, after=last,
        )
        norms = more[0] if first else norms
        last = (state,)
        if side == other:
            behind.send(chunk, state)
        else:
            last = (behind.open(chunk, back_factors, state),)

    parts = {}
    kept = None
    results = []

    def grad_call(side, chunk, after):
        nonlocal kept, results
        flush = kept is not None
        outs = call(
            functools.partial(grad_kernel, done=kept[0] if flush else None, **spots[side, chunk]), "local_grads",
            [column_values, grown, queries[side], keys[side], values[side], grads[side, chunk],
             raws[side, chunk], gain, norms, starts[side, chunk], locals_[side, chunk][3], ready[side, chunk][2], *locals_[side, chunk][4:],
             *(kept[1] if flush else [])],
            [result] * (2 * flush) + [held(part)] * 4, (),
            [pltpu.VMEM((2, BLOCK, MIDDLE), BF16)] + [pull_sems] * flush, after, results,
        )
        if flush:
            results = outs[:2]
        kept = ((side, chunk), outs[-4:-2])
        parts[side, chunk] = outs[-2:]
        return (outs[-1],)

    to_grad = list(order)
    last = grad_call(*to_grad.pop(0), last)
    for stage in range(1, stages):
        for chunk in range(chunks):
            if to_ready:
                last = ready_call(*to_ready.pop(0), last)
            last = (behind.step(chunk, back_factors, last),)
            if to_grad:
                last = grad_call(*to_grad.pop(0), last)
    while to_ready:
        last = ready_call(*to_ready.pop(0), last)
    ends = {}
    for chunk in range(chunks):
        if chunk:
            while to_grad:
                last = grad_call(*to_grad.pop(0), last)
        ends[own, chunk], ends[other, chunk], given = behind.close(chunk, back_factors, last)
        last = (given,)

    def end_call(places, held_ins, done, rest, outs, after, into):
        groups = [[*ready[place][:2], *parts[place], ends[place]] for place in places]
        body = functools.partial(
            end_kernel, heads=heads, spots=places, done=done, rest=rest, scale=1.0 / math.sqrt(positions)
        )
        room = pltpu.VMEM((len(places), *part), BF16)
        return call(
            body, "carried_grads", sum(groups, []) + held_ins, outs, (),
            [room, room, *([pull_sems] * (done is not None)), pltpu.SemaphoreType.DMA((len(places), 2, 2))],
            after, into,
        )

    early = [(own, 0), (other, 0)]
    query_result, attended, *into = end_call(early, list(kept[1]), kept[0], [], [result] * 4, last, results)
    key_result, value_result, gain_result = end_call(
        [(own, 1), (other, 1)], [ends[place] for place in early], None, early,
        [result, result, jax.ShapeDtypeStruct((heads, WIDTH), F32)], (), into,
    )
    return attended, query_result, key_result, value_result, gain_result.reshape(-1)


def solution(mesh):
    in_specs = (
        P("ctx", "dp"),
        P("ctx", "dp"),
        P("ctx", "dp"),
        P("dp", "ctx"),
        P("dp"),
        P("ctx", "dp"),
    )
    out_specs = (P("ctx", "dp"), P("ctx", "dp"), P("ctx", "dp"), P("ctx", "dp"), P("dp"))
    return jax.shard_map(
        on_device, mesh=mesh, in_specs=in_specs, out_specs=out_specs, check_vma=False
    )
```

time: 260 us -> 62.3 us (0.24)
  matrix products: 80.5 us -> 0 us
  blocking collectives: 44 us -> 0 us
  local copies, waits for them, and re-layouts: 44 us -> 0.01 us
  waiting for transfers between devices: 43 us -> 5.09 us
  Pallas kernels: 0 us -> 37.2 us
  other arithmetic: 32.1 us -> 0 us
  starting transfers between devices: 0.08 us -> 18.6 us
  between operations: 14.3 us -> 1.15 us
    dot_general x16 -> x0, matrix products: 80.5 us -> none  [the longest x4 12.6 us: split_product(): jnp.einsum(form, left, low_part, preferred_element_type=jnp.float32)]
    all_gather x2 -> x0, waiting for transfers between devices: 42.9 us -> none  [entering(): pieces = jax.tree.map(lambda part: lax.all_gather(part, axis), value)]
    pallas_call x0 -> x42, Pallas kernels: none -> 37.2 us  [call(): pl.pallas_call(body, name=name, in_specs=[vmem_spec] * len(near) + [any_s...]
    psum x3 -> x0, blocking collectives: 33.8 us -> none  [the longest x2 20.3 us: on_device(): lax.psum((jnp.sum(raw_out * raw_out, axis=1), jnp.sum(scaled_grad * raw_o...]
    select_n x14 -> x0, other arithmetic: 20.4 us -> none  [turn(): jnp.where(position < mine, new, old)]
    ppermute x0 -> x20, starting transfers between devices: none -> 18.6 us  [the longest x12 9.33 us: swap(): lax.ppermute(value, axis, [(i, i ^ bit) for i in range(lax.axis_size(axis...]
    unnamed x28 -> x2, local copies, waits for them, and re-layouts: 16 us -> 0.01 us
    reshape x4 -> x0, local copies, waits for them, and re-layouts: 10.5 us -> none  [the longest x1 5.36 us: on_device(): raw_out = (carried + local_mix).reshape(row_count, -1)]
  transfers between devices with their start and end apart: 2 -> 20, of which waited for: 2 -> 7; matrix products, arithmetic and copies ran while one was open for 17% -> 0% of each run, Pallas kernels for 0% -> 50%
where the time goes in v1:
time: 62.3 us; the launch traced here: 62.1 us
  Pallas kernels  37.2 us (60%)
  starting transfers between devices  18.6 us (30%)
  waiting for transfers between devices  5.09 us (8%)
  between operations  1.15 us (2%)
    pallas_call x42, Pallas kernels, call(): pl.pallas_call(body, name=name, in_specs=[vmem_spec] * len(near) + [any_s...  37.2 us
    ppermute x12, starting transfers between devices, swap(): lax.ppermute(value, axis, [(i, i ^ bit) for i in range(lax.axis_size(axis...  9.33 us
    ppermute x8, starting transfers between devices, forward(): lax.ppermute(message if sent is None else sent, 'ctx', pairs)  9.3 us
    ppermute x8, waiting for transfers between devices, forward(): lax.ppermute(message if sent is None else sent, 'ctx', pairs)  3.91 us
  transfers between devices with their start and end apart: 20, of which 7 were waited for; matrix products, arithmetic and copies ran while one was open for 0% of the time, Pallas kernels for 50%

profile of v1, /device:TPU:0, one launch (start us, length us, event | category | flops | bytes accessed | tf_op | source)
XLA Modules:
  0.0 62.1 jit_solution(15718921836966907540)
XLA Ops:
  0.6 2.3 %first_state.1 = (f32[16,512]{1,0:T(8,128)S(1)}, f32[512,128]{1,0:T(8,128)S(1)}, f32[512,128]{1,0:T(8,128)S(1)}, f32[512,128]{1,0:T(8,128)S(1)}, f32[16,128]{1,0...) custom-call(f32[16,512]{1,0:T(8,128)} %decay_in.1, ...), custom_call_target="tpu_custom_call" | custom-call | flops 10000 | bytes 1024 | tf_op jit(solution)/shard_map/first_state/pallas_call | solution.py:600
  2.9 3.0 %collective-permute-start = (f32[16,128]{1,0:T(8,128)S(1)}, f32[16,128]{1,0:T(8,128)S(1)}, u32[]{:S(2)}, u32[]{:S(2)}) collective-permute-start(f32[16,128]{1,0:T(8,128)S(1)} %get-tuple-element.131.left_ref), channel_id=1, source_target_pairs={{0,8},{4,12},{8,0},{12,4},{16,24},{20,28},{24,16},{28,20},{1,9},{5... | collective-permute-start | bytes 24584 | tf_op jit(solution)/shard_map/ppermute | solution.py:483
  5.9 1.2 %local_state.3 = (f32[512,128]{1,0:T(8,128)S(1)}, bf16[512,1024]{1,0:T(8,128)(2,1)S(1)}) custom-call(f32[512,128]{1,0:T(8,128)S(1)} %get-tuple-element.122.tail_ref, bf16[512,1024]{1,0:T(8,128)(2,1)S(1)} %get-tuple-element.123.key_ref, bf16[512,1024]{1,0:T(8,128)(2,1)S(1)} %get-tuple-element.124.value_ref, bf16[512,2048]{1,0:T(8,128)(2,1)} %refs_0_.4, ...), custom_call_target="tpu_custom_call" | custom-call | flops 10000 | bytes 1024 | tf_op jit(solution)/shard_map/local_state/pallas_call | solution.py:600
  7.2 0.9 %local_state.4.refs_0_.refs_3_ = f32[512,128]{1,0:T(8,128)S(1)} custom-call(f32[512,128]{1,0:T(8,128)S(1)} %get-tuple-element.122.tail_ref, bf16[512,1024]{1,0:T(8,128)(2,1)S(1)} %get-tuple-element.127.key_ref, bf16[512,1024]{1,0:T(8,128)(2,1)S(1)} %get-tuple-element.128.value_ref, f32[512,128]{1,0:T(8,128)S(1)} %get-tuple-element.132.refs_0_.state_ref), custom_call_target="tpu_custom_call" | custom-call | flops 10000 | bytes 1024 | tf_op jit(solution)/shard_map/local_state/pallas_call | solution.py:600
  8.1 0.0 collective-permute-done.right_ref
  8.1 0.6 collective-permute-start.2
  8.7 0.1 collective-permute-start.1
  8.7 1.2 %local_state.5 = (f32[512,128]{1,0:T(8,128)S(1)}, bf16[512,1024]{1,0:T(8,128)(2,1)S(1)}) custom-call(f32[512,128]{1,0:T(8,128)S(1)} %get-tuple-element.122.tail_ref, bf16[512,1024]{1,0:T(8,128)(2,1)S(1)} %get-tuple-element.127.key_ref, bf16[512,1024]{1,0:T(8,128)(2,1)S(1)} %get-tuple-element.128.value_ref, bf16[512,2048]{1,0:T(8,128)(2,1)} %refs_0_.4, ...), custom_call_target="tpu_custom_call" | custom-call | flops 10000 | bytes 1024 | tf_op jit(solution)/shard_map/local_state/pallas_call | solution.py:600
  10.0 0.1 factors.2.factor_ref
  10.1 0.1 blend.12
  10.2 1.5 %collective-permute-start.4 = (f32[512,128]{1,0:T(8,128)S(1)}, f32[512,128]{1,0:T(8,128)S(1)}, u32[]{:S(2)}, u32[]{:S(2)}) collective-permute-start(f32[512,128]{1,0:T(8,128)S(1)} %get-tuple-element.142), channel_id=1, source_target_pairs={{0,8},{4,20},{8,0},{12,28},{16,24},{20,4},{24,16},{28,12},{1,9},{5... | collective-permute-start | bytes 786440 | tf_op jit(solution)/shard_map/ppermute | solution.py:633
  11.7 0.0 collective-permute-done.2.refs_1_.refs_2_
  11.7 0.1 blend.13
  11.8 0.7 %collective-permute-start.6 = (f32[512,128]{1,0:T(8,128)S(1)}, f32[512,128]{1,0:T(8,128)S(1)}, u32[]{:S(2)}, u32[]{:S(2)}) collective-permute-start(f32[512,128]{1,0:T(8,128)S(1)} %get-tuple-element.143), channel_id=1, source_target_pairs={{0,8},{4,20},{8,0},{12,28},{16,24},{20,4},{24,16},{28,12},{1,9},{5... | collective-permute-start | bytes 786440 | tf_op jit(solution)/shard_map/ppermute | solution.py:633
  12.4 2.3 %local_mix.4 = (bf16[512,512]{1,0:T(8,128)(2,1)S(1)}, bf16[512,512]{1,0:T(8,128)(2,1)S(1)}, bf16[512,512]{1,0:T(8,128)(2,1)S(1)}, bf16[4,128,128]{2,1,0:T(8,128)...) custom-call(f32[16,512]{1,0:T(8,128)S(1)} %get-tuple-element.129.row, ...), custom_call_target="tpu_custom_call" | custom-call | flops 10000 | bytes 1024 | tf_op jit(solution)/shard_map/local_mix/pallas_call | solution.py:600
  14.8 1.9 %collective-permute-done.4.refs_1_.refs_0_ = f32[512,128]{1,0:T(8,128)S(1)} collective-permute-done((f32[512,128]{1,0:T(8,128)S(1)}, f32[512,128]{1,0:T(8,128)S(1)}, u32[]{:S(2)}, u32[]{:S(2)}) %collective-permute-start.4) | collective-permute-done | bytes 262176 | tf_op jit(solution)/shard_map/ppermute | solution.py:633
  16.7 1.6 %collective-permute-start.5 = (f32[512,128]{1,0:T(8,128)S(1)}, f32[512,128]{1,0:T(8,128)S(1)}, u32[]{:S(2)}, u32[]{:S(2)}) collective-permute-start(f32[512,128]{1,0:T(8,128)S(1)} %blend.14.refs_0_.refs_4_), channel_id=1, source_target_pairs={{0,16},{4,12},{8,24},{12,4},{16,0},{20,28},{24,8},{28,20},{1,17},{... | collective-permute-start | bytes 786440 | tf_op jit(solution)/shard_map/ppermute | solution.py:633
  18.2 2.3 %local_mix.5 = (bf16[512,512]{1,0:T(8,128)(2,1)S(1)}, bf16[512,512]{1,0:T(8,128)(2,1)S(1)}, bf16[512,512]{1,0:T(8,128)(2,1)S(1)}, bf16[4,128,128]{2,1,0:T(8,128)...) custom-call(f32[16,512]{1,0:T(8,128)S(1)} %get-tuple-element.129.row_ref, ...), custom_call_target="tpu_custom_call" | custom-call | flops 10000 | bytes 1024 | tf_op jit(solution)/shard_map/local_mix/pallas_call | solution.py:600
  20.6 1.0 %collective-permute-start.7 = (f32[512,128]{1,0:T(8,128)S(1)}, f32[512,128]{1,0:T(8,128)S(1)}, u32[]{:S(2)}, u32[]{:S(2)}) collective-permute-start(f32[512,128]{1,0:T(8,128)S(1)} %blend.15.refs_0_.refs_4_), channel_id=1, source_target_pairs={{0,16},{4,12},{8,24},{12,4},{16,0},{20,28},{24,8},{28,20},{1,17},{... | collective-permute-start | bytes 786440 | tf_op jit(solution)/shard_map/ppermute | solution.py:633
  21.5 2.3 %local_mix.6 = (bf16[512,512]{1,0:T(8,128)(2,1)S(1)}, bf16[512,512]{1,0:T(8,128)(2,1)S(1)}, bf16[512,512]{1,0:T(8,128)(2,1)S(1)}, bf16[4,128,128]{2,1,0:T(8,128)...) custom-call(f32[16,512]{1,0:T(8,128)S(1)} %get-tuple-element.129.row_ref, ...), custom_call_target="tpu_custom_call" | custom-call | flops 10000 | bytes 1024 | tf_op jit(solution)/shard_map/local_mix/pallas_call | solution.py:600
  23.8 0.1 factors.3.refs_5_.factor_ref
  23.9 0.1 blend.16
  24.0 0.1 collective-permute-start.9
  24.1 0.4 raw_out.4
  24.6 2.5 %local_mix.7 = (bf16[512,512]{1,0:T(8,128)(2,1)S(1)}, bf16[512,512]{1,0:T(8,128)(2,1)S(1)}, bf16[512,512]{1,0:T(8,128)(2,1)S(1)}, bf16[4,128,128]{2,1,0:T(8,128)...) custom-call(f32[16,512]{1,0:T(8,128)S(1)} %get-tuple-element.129.row_ref, ...), custom_call_target="tpu_custom_call" | custom-call | flops 10000 | bytes 1024 | tf_op jit(solution)/shard_map/local_mix/pallas_call | solution.py:600
  27.1 0.1 blend.17
  27.2 0.6 collective-permute-start.8
  27.7 0.5 raw_out.5
  28.2 0.5 raw_out.6
  28.7 0.2 collective-permute-done.8.start_ref
  28.9 0.6 raw_out.7
  29.5 1.7 %collective-permute-start.10 = (f32[2,512]{1,0:T(2,128)S(1)}, f32[2,512]{1,0:T(2,128)S(1)}, u32[]{:S(2)}, u32[]{:S(2)}) collective-permute-start(f32[2,512]{1,0:T(2,128)S(1)} %get-tuple-element.158.refs_0_.left_ref), channel_id=1, source_target_pairs={{0,1},{1,0},{2,3},{3,2},{4,5},{5,4},{6,7},{7,6},{8,9},{9,8},{10,11... | collective-permute-start | bytes 12296 | tf_op jit(solution)/shard_map/ppermute | solution.py:483
  31.1 0.7 %weighted.4 = (bf16[512,512]{1,0:T(8,128)(2,1)S(1)}, bf16[512,512]{1,0:T(8,128)(2,1)S(1)}, bf16[512,256]{1,0:T(8,128)(2,1)S(1)}) custom-call(f32[512,128]{1,0:T(8,128)S(1)} %get-tuple-element.121.column_ref, f32[512,128]{1,0:T(8,128)S(1)} %get-tuple-element.122.tail_ref, bf16[512,1024]{1,0:T(8,128)(2,1)S(1)} %get-tuple-element.126.query_ref, ...), custom_call_target="tpu_custom_call" | custom-call | flops 10000 | bytes 1024 | tf_op jit(solution)/shard_map/weighted/pallas_call | solution.py:600
  31.9 0.8 %weighted.5 = (bf16[512,512]{1,0:T(8,128)(2,1)S(1)}, bf16[512,512]{1,0:T(8,128)(2,1)S(1)}, bf16[512,256]{1,0:T(8,128)(2,1)S(1)}) custom-call(f32[512,128]{1,0:T(8,128)S(1)} %get-tuple-element.121.column_ref, f32[512,128]{1,0:T(8,128)S(1)} %get-tuple-element.122.tail_ref, bf16[512,1024]{1,0:T(8,128)(2,1)S(1)} %get-tuple-element.126.query_ref, ...), custom_call_target="tpu_custom_call" | custom-call | flops 10000 | bytes 1024 | tf_op jit(solution)/shard_map/weighted/pallas_call | solution.py:600
  32.6 0.5 collective-permute-done.10.right_ref
  33.2 2.6 %collective-permute-start.11 = (f32[2,512]{1,0:T(2,128)S(1)}, f32[2,512]{1,0:T(2,128)S(1)}, u32[]{:S(2)}, u32[]{:S(2)}) collective-permute-start(f32[2,512]{1,0:T(2,128)S(1)} %sums.1.refs_0_.sums_ref), channel_id=1, source_target_pairs={{0,2},{1,3},{2,0},{3,1},{4,6},{5,7},{6,4},{7,5},{8,10},{9,11},{10,... | collective-permute-start | bytes 12296 | tf_op jit(solution)/shard_map/ppermute | solution.py:483
  35.8 0.7 %weighted.6 = (bf16[512,512]{1,0:T(8,128)(2,1)S(1)}, bf16[512,512]{1,0:T(8,128)(2,1)S(1)}, bf16[512,256]{1,0:T(8,128)(2,1)S(1)}) custom-call(f32[512,128]{1,0:T(8,128)S(1)} %get-tuple-element.121.column_ref, f32[512,128]{1,0:T(8,128)S(1)} %get-tuple-element.122.tail_ref, bf16[512,1024]{1,0:T(8,128)(2,1)S(1)} %get-tuple-element.134.query_ref, ...), custom_call_target="tpu_custom_call" | custom-call | flops 10000 | bytes 1024 | tf_op jit(solution)/shard_map/weighted/pallas_call | solution.py:600
  36.5 0.8 %weighted.7 = (bf16[512,512]{1,0:T(8,128)(2,1)S(1)}, bf16[512,512]{1,0:T(8,128)(2,1)S(1)}, bf16[512,256]{1,0:T(8,128)(2,1)S(1)}) custom-call(f32[512,128]{1,0:T(8,128)S(1)} %get-tuple-element.121.column_ref, f32[512,128]{1,0:T(8,128)S(1)} %get-tuple-element.122.tail_ref, bf16[512,1024]{1,0:T(8,128)(2,1)S(1)} %get-tuple-element.134.query_ref, ...), custom_call_target="tpu_custom_call" | custom-call | flops 10000 | bytes 1024 | tf_op jit(solution)/shard_map/weighted/pallas_call | solution.py:600
  37.3 0.4 collective-permute-done.11.refs_0_
  37.7 0.8 %grad_raw.4 = (bf16[512,512]{1,0:T(8,128)(2,1)S(1)}, f32[520,128]{1,0:T(8,128)S(1)}, f32[2,512,128]{2,1,0:T(8,128)S(1)}) custom-call(bf16[512,512]{1,0:T(8,128)(2,1)S(1)} %get-tuple-element.163.turned_ref, bf16[512,512]{1,0:T(8,128)(2,1)S(1)} %get-tuple-element.164.raw_ref, bf16[512,1024]{1,0:T(8,128)(2,1)S(1)} %get-tuple-element.151.grad_ref, ...), custom_call_target="tpu_custom_call" | custom-call | flops 10000 | bytes 1024 | tf_op jit(solution)/shard_map/grad_raw/pallas_call | solution.py:600
  38.5 0.1 collective-permute-start.12
  38.5 0.6 %grad_raw.5 = (bf16[512,512]{1,0:T(8,128)(2,1)S(1)}, f32[520,128]{1,0:T(8,128)S(1)}) custom-call(bf16[512,512]{1,0:T(8,128)(2,1)S(1)} %get-tuple-element.169.turned_ref, bf16[512,512]{1,0:T(8,128)(2,1)S(1)} %get-tuple-element.170.raw_ref, bf16[512,1024]{1,0:T(8,128)(2,1)S(1)} %get-tuple-element.151.grad_ref, f32[1,2048]{1,0:T(1,128)S(1)} %bitcast.7, ...), custom_call_target="tpu_custom_call" | custom-call | flops 10000 | bytes 1024 | tf_op jit(solution)/shard_map/grad_raw/pallas_call | solution.py:600
  39.2 0.6 collective-permute-start.13
  39.7 0.6 %grad_raw.6 = (bf16[512,512]{1,0:T(8,128)(2,1)S(1)}, f32[520,128]{1,0:T(8,128)S(1)}) custom-call(bf16[512,512]{1,0:T(8,128)(2,1)S(1)} %get-tuple-element.161.turned_ref, bf16[512,512]{1,0:T(8,128)(2,1)S(1)} %get-tuple-element.162.raw_ref, bf16[512,1024]{1,0:T(8,128)(2,1)S(1)} %get-tuple-element.141.grad_ref, f32[1,2048]{1,0:T(1,128)S(1)} %bitcast.8, ...), custom_call_target="tpu_custom_call" | custom-call | flops 10000 | bytes 1024 | tf_op jit(solution)/shard_map/grad_raw/pallas_call | solution.py:600
  40.4 0.1 blend.18
  40.4 1.9 %collective-permute-start.14 = (f32[520,128]{1,0:T(8,128)S(1)}, f32[520,128]{1,0:T(8,128)S(1)}, u32[]{:S(2)}, u32[]{:S(2)}) collective-permute-start(f32[520,128]{1,0:T(8,128)S(1)} %get-tuple-element.186), channel_id=1, source_target_pairs={{0,8},{4,20},{8,0},{12,28},{16,24},{20,4},{24,16},{28,12},{1,9},{5... | collective-permute-start | bytes 798728 | tf_op jit(solution)/shard_map/ppermute | solution.py:633
  42.3 0.6 %grad_raw.7 = (bf16[512,512]{1,0:T(8,128)(2,1)S(1)}, f32[520,128]{1,0:T(8,128)S(1)}) custom-call(bf16[512,512]{1,0:T(8,128)(2,1)S(1)} %get-tuple-element.178.turned_ref, bf16[512,512]{1,0:T(8,128)(2,1)S(1)} %get-tuple-element.179.raw_ref, bf16[512,1024]{1,0:T(8,128)(2,1)S(1)} %get-tuple-element.141.grad_ref, f32[1,2048]{1,0:T(1,128)S(1)} %bitcast.9, ...), custom_call_target="tpu_custom_call" | custom-call | flops 10000 | bytes 1024 | tf_op jit(solution)/shard_map/grad_raw/pallas_call | solution.py:600
  43.0 0.1 blend.19
  43.0 0.3 collective-permute-start.16
  43.3 2.2 %local_grads.4 = (bf16[512,512]{1,0:T(8,128)(2,1)S(1)}, bf16[512,512]{1,0:T(8,128)(2,1)S(1)}, bf16[512,512]{1,0:T(8,128)(2,1)S(1)}, bf16[512,512]{1,0:T(8,128)(2,1)S(1)}) custom-call(f32[512,128]{1,0:T(8,128)S(1)} %get-tuple-element.121.column_ref, f32[512,128]{1,0:T(8,128)S(1)} %get-tuple-element.130.grown_ref, ...), custom_call_target="tpu_custom_call" | custom-call | flops 10000 | bytes 1024 | tf_op jit(solution)/shard_map/local_grads/pallas_call | solution.py:600
  45.6 1.4 %collective-permute-done.14.refs_1_.refs_0_ = f32[520,128]{1,0:T(8,128)S(1)} collective-permute-done((f32[520,128]{1,0:T(8,128)S(1)}, f32[520,128]{1,0:T(8,128)S(1)}, u32[]{:S(2)}, u32[]{:S(2)}) %collective-permute-start.14) | collective-permute-done | bytes 266272 | tf_op jit(solution)/shard_map/ppermute | solution.py:633
  47.0 1.2 %collective-permute-start.15 = (f32[520,128]{1,0:T(8,128)S(1)}, f32[520,128]{1,0:T(8,128)S(1)}, u32[]{:S(2)}, u32[]{:S(2)}) collective-permute-start(f32[520,128]{1,0:T(8,128)S(1)} %blend.20.refs_2_.refs_4_), channel_id=1, source_target_pairs={{0,16},{4,12},{8,24},{12,4},{16,0},{20,28},{24,8},{28,20},{1,17},{... | collective-permute-start | bytes 798728 | tf_op jit(solution)/shard_map/ppermute | solution.py:633
  48.2 2.3 %local_grads.5 = (bf16[512,2048]{1,0:T(8,128)(2,1)}, bf16[512,2048]{1,0:T(8,128)(2,1)}, bf16[512,512]{1,0:T(8,128)(2,1)S(1)}, bf16[512,512]{1,0:T(8,128)(2,1)S(1...) custom-call(f32[512,128]{1,0:T(8,128)S(1)} %get-tuple-element.121.column_ref, ...), custom_call_target="tpu_custom_call" | custom-call | flops 10000 | bytes 1024 | tf_op jit(solution)/shard_map/local_grads/pallas_call | solution.py:600
  50.4 0.2 collective-permute-done.16.refs_1_.refs_0_
  50.7 1.2 %collective-permute-start.18 = (f32[520,128]{1,0:T(8,128)S(1)}, f32[520,128]{1,0:T(8,128)S(1)}, u32[]{:S(2)}, u32[]{:S(2)}) collective-permute-start(f32[520,128]{1,0:T(8,128)S(1)} %blend.21.refs_4_), channel_id=1, source_target_pairs={{0,16},{4,12},{8,24},{12,4},{16,0},{20,28},{24,8},{28,20},{1,17},{... | collective-permute-start | bytes 798728 | tf_op jit(solution)/shard_map/ppermute | solution.py:633
  51.9 2.3 %local_grads.6 = (bf16[512,2048]{1,0:T(8,128)(2,1)}, bf16[512,2048]{1,0:T(8,128)(2,1)}, bf16[512,512]{1,0:T(8,128)(2,1)S(1)}, bf16[512,512]{1,0:T(8,128)(2,1)S(1...) custom-call(f32[512,128]{1,0:T(8,128)S(1)} %get-tuple-element.121.co, ...), custom_call_target="tpu_custom_call", output_to_operand_aliasing={{0}: (16, {}), {1}: (17, {})} | custom-call | flops 10000 | bytes 1024 | tf_op jit(solution)/shard_map/local_grads/pallas_call | solution.py:600
  54.2 0.1 blend.22
  54.4 0.1 collective-permute-start.17
  54.4 2.3 %local_grads.7 = (bf16[512,2048]{1,0:T(8,128)(2,1)}, bf16[512,2048]{1,0:T(8,128)(2,1)}, bf16[512,512]{1,0:T(8,128)(2,1)S(1)}, bf16[512,512]{1,0:T(8,128)(2,1)S(1...) custom-call(f32[512,128]{1,0:T(8,128)S(1)} %get-tuple-element.121.co, ...), custom_call_target="tpu_custom_call", output_to_operand_aliasing={{0}: (16, {}), {1}: (17, {})} | custom-call | flops 10000 | bytes 1024 | tf_op jit(solution)/shard_map/local_grads/pallas_call | solution.py:600
  56.7 0.4 collective-permute-done.18.refs_1_
  57.2 0.1 blend.23
  57.3 0.1 collective-permute-start.19
  57.4 1.9 %carried_grads.2 = (bf16[512,2048]{1,0:T(8,128)(2,1)}, bf16[512,2048]{1,0:T(8,128)(2,1)}, bf16[512,2048]{1,0:T(8,128)(2,1)}, bf16[512,2048]{1,0:T(8,128)(2,1)}) custom-call(bf16[512,512]{1,0:T(8,128)(2,1)S(1)} %get-tuple-element.159.refs_0_, bf16[512,512]{1,0:T(8,128)(2,1)S(1)} %get-tuple-element.160.refs_1_, ...), custom_call_target="tpu_custom_call", output_to_operand_aliasing={{0}: (12, {}), {1}: (13, {})} | custom-call | flops 10000 | bytes 1024 | tf_op jit(solution)/shard_map/carried_grads/pallas_call | solution.py:600
  59.4 2.5 %carried_grads.3 = (bf16[512,2048]{1,0:T(8,128)(2,1)}, bf16[512,2048]{1,0:T(8,128)(2,1)}, f32[16,128]{1,0:T(8,128)}) custom-call(bf16[512,512]{1,0:T(8,128)(2,1)S(1)} %get-tuple-element.165.refs_0_, bf16[512,512]{1,0:T(8,128)(2,1)S(1)} %get-tuple-element.227.refs_1_, ...), custom_call_target="tpu_custom_call", output_to_operand_aliasing={{0}: (12, {}), {1}: (13, {})} | custom-call | flops 10000 | bytes 1024 | tf_op jit(solution)/shard_map/carried_grads/pallas_call | solution.py:600
  (20 shorter events, 0.2 us)
Async XLA Ops:
  2.9 5.1 %collective-permute-start = (f32[16,128]{1,0:T(8,128)S(1)}, f32[16,128]{1,0:T(8,128)S(1)}, u32[]{:S(2)}, u32[]{:S(2)}) collective-permute-start(f32[16,128]{1,0:T(8,128)S(1)} %get-tuple-element.131.left_ref), channel_id=1, source_target_pairs={{0,8},{4,12},{8,0},{12,4},{16,24},{20,28},{24,16},{28,20},{1,9},{5... | collective-permute-start | bytes 24584 | tf_op jit(solution)/shard_map/ppermute | solution.py:483
  5.9 4.2 %collective-permute-start.3 = (f32[512,128]{1,0:T(8,128)S(1)}, f32[512,128]{1,0:T(8,128)S(1)}, u32[]{:S(2)}, u32[]{:S(2)}) collective-permute-start(f32[512,128]{1,0:T(8,128)S(1)} %get-tuple-element.125.refs_1_), channel_id=1, source_target_pairs={{0,4},{4,0},{8,12},{12,8},{16,20},{20,16},{24,28},{28,24},{1,5},{5... | collective-permute-start | bytes 786440 | tf_op jit(solution)/shard_map/ppermute | solution.py:483
  8.1 3.6 %collective-permute-start.2 = (f32[512,128]{1,0:T(8,128)S(1)}, f32[512,128]{1,0:T(8,128)S(1)}, u32[]{:S(2)}, u32[]{:S(2)}) collective-permute-start(f32[512,128]{1,0:T(8,128)S(1)} %get-tuple-element.136), channel_id=1, source_target_pairs={{0,4},{4,0},{8,12},{12,8},{16,20},{20,16},{24,28},{28,24},{1,5},{5... | collective-permute-start | bytes 786440 | tf_op jit(solution)/shard_map/ppermute | solution.py:483
  8.7 1.3 %collective-permute-start.1 = (f32[16,128]{1,0:T(8,128)S(1)}, f32[16,128]{1,0:T(8,128)S(1)}, u32[]{:S(2)}, u32[]{:S(2)}) collective-permute-start(f32[16,128]{1,0:T(8,128)S(1)} %get-tuple-element.133.refs_1_.refs_0_), channel_id=1, source_target_pairs={{0,4},{4,0},{8,12},{12,8},{16,20},{20,16},{24,28},{28,24},{1,5},{5... | collective-permute-start | bytes 24584 | tf_op jit(solution)/shard_map/ppermute | solution.py:483
  10.2 6.4 %collective-permute-start.4 = (f32[512,128]{1,0:T(8,128)S(1)}, f32[512,128]{1,0:T(8,128)S(1)}, u32[]{:S(2)}, u32[]{:S(2)}) collective-permute-start(f32[512,128]{1,0:T(8,128)S(1)} %get-tuple-element.142), channel_id=1, source_target_pairs={{0,8},{4,20},{8,0},{12,28},{16,24},{20,4},{24,16},{28,12},{1,9},{5... | collective-permute-start | bytes 786440 | tf_op jit(solution)/shard_map/ppermute | solution.py:633
  11.8 8.7 %collective-permute-start.6 = (f32[512,128]{1,0:T(8,128)S(1)}, f32[512,128]{1,0:T(8,128)S(1)}, u32[]{:S(2)}, u32[]{:S(2)}) collective-permute-start(f32[512,128]{1,0:T(8,128)S(1)} %get-tuple-element.143), channel_id=1, source_target_pairs={{0,8},{4,20},{8,0},{12,28},{16,24},{20,4},{24,16},{28,12},{1,9},{5... | collective-permute-start | bytes 786440 | tf_op jit(solution)/shard_map/ppermute | solution.py:633
  16.7 7.3 %collective-permute-start.5 = (f32[512,128]{1,0:T(8,128)S(1)}, f32[512,128]{1,0:T(8,128)S(1)}, u32[]{:S(2)}, u32[]{:S(2)}) collective-permute-start(f32[512,128]{1,0:T(8,128)S(1)} %blend.14.refs_0_.refs_4_), channel_id=1, source_target_pairs={{0,16},{4,12},{8,24},{12,4},{16,0},{20,28},{24,8},{28,20},{1,17},{... | collective-permute-start | bytes 786440 | tf_op jit(solution)/shard_map/ppermute | solution.py:633
  20.6 6.5 %collective-permute-start.7 = (f32[512,128]{1,0:T(8,128)S(1)}, f32[512,128]{1,0:T(8,128)S(1)}, u32[]{:S(2)}, u32[]{:S(2)}) collective-permute-start(f32[512,128]{1,0:T(8,128)S(1)} %blend.15.refs_0_.refs_4_), channel_id=1, source_target_pairs={{0,16},{4,12},{8,24},{12,4},{16,0},{20,28},{24,8},{28,20},{1,17},{... | collective-permute-start | bytes 786440 | tf_op jit(solution)/shard_map/ppermute | solution.py:633
  21.5 2.6 %copy-start = (f32[2048]{0:T(1024)S(1)}, f32[2048]{0:T(1024)}, u32[]{:S(2)}) copy-start(f32[2048]{0:T(1024)} %param.10) | copy-start | bytes 24580
  24.0 4.2 %collective-permute-start.9 = (f32[512,128]{1,0:T(8,128)S(1)}, f32[512,128]{1,0:T(8,128)S(1)}, u32[]{:S(2)}, u32[]{:S(2)}) collective-permute-start(f32[512,128]{1,0:T(8,128)S(1)} %get-tuple-element.147.refs_0_), channel_id=1, source_target_pairs={{0,4},{4,0},{8,12},{12,8},{16,20},{20,16},{24,28},{28,24},{1,5},{5... | collective-permute-start | bytes 786440 | tf_op jit(solution)/shard_map/ppermute | solution.py:483
  27.2 1.7 %collective-permute-start.8 = (f32[512,128]{1,0:T(8,128)S(1)}, f32[512,128]{1,0:T(8,128)S(1)}, u32[]{:S(2)}, u32[]{:S(2)}) collective-permute-start(f32[512,128]{1,0:T(8,128)S(1)} %get-tuple-element.152.refs_1_), channel_id=1, source_target_pairs={{0,4},{4,0},{8,12},{12,8},{16,20},{20,16},{24,28},{28,24},{1,5},{5... | collective-permute-start | bytes 786440 | tf_op jit(solution)/shard_map/ppermute | solution.py:483
  29.5 3.7 %collective-permute-start.10 = (f32[2,512]{1,0:T(2,128)S(1)}, f32[2,512]{1,0:T(2,128)S(1)}, u32[]{:S(2)}, u32[]{:S(2)}) collective-permute-start(f32[2,512]{1,0:T(2,128)S(1)} %get-tuple-element.158.refs_0_.left_ref), channel_id=1, source_target_pairs={{0,1},{1,0},{2,3},{3,2},{4,5},{5,4},{6,7},{7,6},{8,9},{9,8},{10,11... | collective-permute-start | bytes 12296 | tf_op jit(solution)/shard_map/ppermute | solution.py:483
  33.2 4.5 %collective-permute-start.11 = (f32[2,512]{1,0:T(2,128)S(1)}, f32[2,512]{1,0:T(2,128)S(1)}, u32[]{:S(2)}, u32[]{:S(2)}) collective-permute-start(f32[2,512]{1,0:T(2,128)S(1)} %sums.1.refs_0_.sums_ref), channel_id=1, source_target_pairs={{0,2},{1,3},{2,0},{3,1},{4,6},{5,7},{6,4},{7,5},{8,10},{9,11},{10,... | collective-permute-start | bytes 12296 | tf_op jit(solution)/shard_map/ppermute | solution.py:483
  38.5 1.9 %collective-permute-start.12 = (f32[520,128]{1,0:T(8,128)S(1)}, f32[520,128]{1,0:T(8,128)S(1)}, u32[]{:S(2)}, u32[]{:S(2)}) collective-permute-start(f32[520,128]{1,0:T(8,128)S(1)} %get-tuple-element.171.refs_0_), channel_id=1, source_target_pairs={{0,4},{4,0},{8,12},{12,8},{16,20},{20,16},{24,28},{28,24},{1,5},{5... | collective-permute-start | bytes 798728 | tf_op jit(solution)/shard_map/ppermute | solution.py:483
  39.2 3.8 %collective-permute-start.13 = (f32[520,128]{1,0:T(8,128)S(1)}, f32[520,128]{1,0:T(8,128)S(1)}, u32[]{:S(2)}, u32[]{:S(2)}) collective-permute-start(f32[520,128]{1,0:T(8,128)S(1)} %get-tuple-element.172.refs_0_), channel_id=1, source_target_pairs={{0,4},{4,0},{8,12},{12,8},{16,20},{20,16},{24,28},{28,24},{1,5},{5... | collective-permute-start | bytes 798728 | tf_op jit(solution)/shard_map/ppermute | solution.py:483
  40.4 6.5 %collective-permute-start.14 = (f32[520,128]{1,0:T(8,128)S(1)}, f32[520,128]{1,0:T(8,128)S(1)}, u32[]{:S(2)}, u32[]{:S(2)}) collective-permute-start(f32[520,128]{1,0:T(8,128)S(1)} %get-tuple-element.186), channel_id=1, source_target_pairs={{0,8},{4,20},{8,0},{12,28},{16,24},{20,4},{24,16},{28,12},{1,9},{5... | collective-permute-start | bytes 798728 | tf_op jit(solution)/shard_map/ppermute | solution.py:633
  43.0 7.6 %collective-permute-start.16 = (f32[520,128]{1,0:T(8,128)S(1)}, f32[520,128]{1,0:T(8,128)S(1)}, u32[]{:S(2)}, u32[]{:S(2)}) collective-permute-start(f32[520,128]{1,0:T(8,128)S(1)} %get-tuple-element.203), channel_id=1, source_target_pairs={{0,8},{4,20},{8,0},{12,28},{16,24},{20,4},{24,16},{28,12},{1,9},{5... | collective-permute-start | bytes 798728 | tf_op jit(solution)/shard_map/ppermute | solution.py:633
  47.0 7.2 %collective-permute-start.15 = (f32[520,128]{1,0:T(8,128)S(1)}, f32[520,128]{1,0:T(8,128)S(1)}, u32[]{:S(2)}, u32[]{:S(2)}) collective-permute-start(f32[520,128]{1,0:T(8,128)S(1)} %blend.20.refs_2_.refs_4_), channel_id=1, source_target_pairs={{0,16},{4,12},{8,24},{12,4},{16,0},{20,28},{24,8},{28,20},{1,17},{... | collective-permute-start | bytes 798728 | tf_op jit(solution)/shard_map/ppermute | solution.py:633
  50.7 6.5 %collective-permute-start.18 = (f32[520,128]{1,0:T(8,128)S(1)}, f32[520,128]{1,0:T(8,128)S(1)}, u32[]{:S(2)}, u32[]{:S(2)}) collective-permute-start(f32[520,128]{1,0:T(8,128)S(1)} %blend.21.refs_4_), channel_id=1, source_target_pairs={{0,16},{4,12},{8,24},{12,4},{16,0},{20,28},{24,8},{28,20},{1,17},{... | collective-permute-start | bytes 798728 | tf_op jit(solution)/shard_map/ppermute | solution.py:633
  54.4 3.1 %collective-permute-start.17 = (f32[520,128]{1,0:T(8,128)S(1)}, f32[520,128]{1,0:T(8,128)S(1)}, u32[]{:S(2)}, u32[]{:S(2)}) collective-permute-start(f32[520,128]{1,0:T(8,128)S(1)} %get-tuple-element.209.refs_4_), channel_id=1, source_target_pairs={{0,4},{4,0},{8,12},{12,8},{16,20},{20,16},{24,28},{28,24},{1,5},{5... | collective-permute-start | bytes 798728 | tf_op jit(solution)/shard_map/ppermute | solution.py:483
  57.3 2.1 %collective-permute-start.19 = (f32[520,128]{1,0:T(8,128)S(1)}, f32[520,128]{1,0:T(8,128)S(1)}, u32[]{:S(2)}, u32[]{:S(2)}) collective-permute-start(f32[520,128]{1,0:T(8,128)S(1)} %get-tuple-element.224.refs_14_), channel_id=1, source_target_pairs={{0,4},{4,0},{8,12},{12,8},{16,20},{20,16},{24,28},{28,24},{1,5},{5... | collective-permute-start | bytes 798728 | tf_op jit(solution)/shard_map/ppermute | solution.py:483
